TPU v7x, 32 devices: a whole 2x2x4 slice. The times are simulated.
32 devices in a mesh: groups: 2 (over x), ctx: 16 (over z, y, core).
Axes of the slice: x: 2, y: 2, z: 4, core: 2. Of those that a mesh axis runs over, the one named last changes fastest.
Arguments:
- queries: bfloat16 [4096, 4096], P(('groups', 'ctx')), parts along dimension 0, may hold values from -12 to 12
- keys: bfloat16 [4096, 512], P(('groups', 'ctx')), parts along dimension 0, may hold values from -9 to 9
- values: bfloat16 [4096, 512], P(('groups', 'ctx')), parts along dimension 0, may hold values from -6 to 6
- doc_lengths: int32 [32], P('groups'), parts along dimension 0, may hold values from 1 to 1024, 2048 in all
Outputs:
- attended: bfloat16 [4096, 4096], P(('groups', 'ctx')), parts along dimension 0
There are 2 independent parts, one for each index of `groups`. A program takes and returns all parts, laid end to end along the dimension named above; each array names one. Nothing has to cross between parts.
Inputs may be any that keep to these rules, and one draw needn't show every extreme that they name: `doc_lengths`: the lengths sum to 2048, and the longest document has exactly 1024 tokens.
All inputs are finite; a program needn't handle non-finite values.
Results may differ from a plain program's by a relative error of at most 0.003.
Values may be sent and summed in bfloat16 or wider, within the bound.
No kernel may reach another device: no remote copies, remote signals or barrier semaphores. Data moves between devices by JAX's collectives and lax.ppermute only.
A program may use at most 128 MiB of HBM per device.

v0:
```python
import functools
import math

import jax
import jax.numpy as jnp
from jax import lax
from jax.experimental import pallas as pl
from jax.experimental.pallas import tpu as pltpu
from jax.sharding import PartitionSpec as P

HEADS = 32
KV_HEADS = 4
HEAD_DIM = 128
GROUP = HEADS // KV_HEADS
NEG = -1e30
EXP2_SCALE = math.log2(math.e) / math.sqrt(HEAD_DIM)


def document_starts(doc_ref, position):
    start = jnp.zeros_like(position)
    end = jnp.int32(0)
    for d in range(doc_ref.shape[0]):
        end = end + doc_ref[d]
        start = jnp.where(position >= end, end, start)
    return start


def attend_kernel(first, last, offsets, picks, plane, *refs):
    n_pairs = max(max(p) for p in picks) + 1
    doc_ref, q_ref = refs[:2]
    kv_refs = refs[2 : 2 + 2 * n_pairs]
    rest = refs[2 + 2 * n_pairs :]
    if first:
        rest = (None, None) + rest
    acc_in, ml_in = rest[:2]
    rest = rest[2:]
    rows = q_ref.shape[0]
    me = lax.axis_index("ctx")
    chip, core = me // 2, me % 2
    odd = chip % 2 == 1
    lane = lax.broadcasted_iota(jnp.int32, (rows, rows), 1)
    position = me * rows + lax.broadcasted_iota(jnp.int32, (rows, rows), 0)
    start = document_starts(doc_ref, position)
    biases = []
    for offset in offsets:
        for other in (0, 1):
            block = 2 * (chip - offset) + (core if other == 0 else 1 - core)
            key = block * rows + lane
            biases.append(jnp.where((key >= start) & (key <= position), 0.0, NEG))
    bias = jnp.concatenate(biases, axis=1)
    keys = bias.shape[1]
    ones = jnp.ones((keys, HEAD_DIM), jnp.bfloat16)

    def columns(column):
        tiles = []
        for even_pick, odd_pick in picks:
            for other in (0, 1):
                at = pl.ds(pl.multiple_of(column * HEAD_DIM, HEAD_DIM), HEAD_DIM)
                tile = kv_refs[2 * even_pick + other][:, at]
                if odd_pick != even_pick:
                    tile = jnp.where(odd, kv_refs[2 * odd_pick + other][:, at], tile)
                tiles.append(tile)
        return jnp.concatenate(tiles, axis=0)

    def body(j, carry):
        key_tile = columns(j)
        value_tile = jnp.concatenate([columns(KV_HEADS + j), ones], axis=1)
        ml_new = jnp.zeros((rows, HEAD_DIM), jnp.float32)
        for g in range(GROUP):
            at = pl.ds(pl.multiple_of((j * GROUP + g) * HEAD_DIM, HEAD_DIM), HEAD_DIM)
            scores = lax.dot_general(
                q_ref[:, at], key_tile, (((1,), (1,)), ((), ())), preferred_element_type=jnp.float32
            )
            scores = scores + bias
            top = jnp.max(scores, axis=1, keepdims=True)
            if not first:
                top_before = ml_in[j][:, g : g + 1]
                total_before = ml_in[j][:, GROUP + g : GROUP + g + 1]
                top = jnp.maximum(top, top_before)
            weights = jnp.exp2((scores - top) * EXP2_SCALE).astype(jnp.bfloat16)
            both = jnp.dot(weights, value_tile, preferred_element_type=jnp.float32)
            acc, total = both[:, :HEAD_DIM], both[:, HEAD_DIM:]
            if not first:
                fade = jnp.exp2((top_before - top) * EXP2_SCALE)
                acc = acc + acc_in[:, at] * fade
                total = total + total_before * fade
            if last:
                rest[0][:, at] = (acc / total).astype(jnp.bfloat16)
            else:
                rest[0][:, at] = acc
                ml_new = jnp.where(lane == g, top, ml_new)
                ml_new = jnp.where(lane == GROUP + g, total, ml_new)
        if not last:
            rest[1][j] = ml_new
        return carry

    lax.fori_loop(0, KV_HEADS, body, 0)


def attend(doc_lengths, queries, pairs, offsets, picks, plane, state=None, last=True):
    rows = queries.shape[0]
    first = state is None
    operands = [doc_lengths, queries] + [block for pair in pairs for block in pair] + list(state or ())
    vmem = pl.BlockSpec(memory_space=pltpu.VMEM)
    in_specs = [pl.BlockSpec(memory_space=pltpu.SMEM)] + [vmem] * (len(operands) - 1)
    if last:
        out_shape = jax.ShapeDtypeStruct(queries.shape, jnp.bfloat16)
        out_specs = vmem
    else:
        out_shape = (
            jax.ShapeDtypeStruct(queries.shape, jnp.float32),
            jax.ShapeDtypeStruct((KV_HEADS, rows, HEAD_DIM), jnp.float32),
        )
        out_specs = (vmem, vmem)
    keys = 2 * rows * len(offsets)
    return pl.pallas_call(
        functools.partial(attend_kernel, first, last, offsets, picks, plane),
        out_shape=out_shape,
        in_specs=in_specs,
        out_specs=out_specs,
        compiler_params=pltpu.CompilerParams(vmem_limit_bytes=40 * 1024 * 1024),
        cost_estimate=pl.CostEstimate(
            flops=4 * rows * HEADS * HEAD_DIM * keys,
            bytes_accessed=queries.size * 4 + keys * 2 * KV_HEADS * HEAD_DIM * 2,
            transcendentals=rows * HEADS * keys,
        ),
    )(*operands)


def local(n, queries, keys, values, doc_lengths):
    plane = 4
    reach = n // 2 // plane

    def swap(x, bit):
        return lax.ppermute(x, "ctx", [(i, i ^ bit) for i in range(n)])

    def onward(x):
        return lax.ppermute(x, "ctx", [(i, (i + plane) % n) for i in range(n)])

    column = [jnp.concatenate([keys, values], axis=1)]
    for _ in range(reach):
        column.append(onward(column[-1]))
    across = [swap(x, 2) for x in column]
    column = [(x, swap(x, 1)) for x in column]
    across = [(x, swap(x, 1)) for x in across]

    early_pairs = column[:reach] + across[:reach]
    early_offsets, early_picks = [], []
    for d in range(reach):
        early_offsets.append(2 * d)
        early_picks.append((d, d))
        if d > 0:
            early_offsets.append(2 * d - 1)
            early_picks.append((reach + d, reach + d - 1))
    state = attend(doc_lengths, queries, early_pairs, early_offsets, early_picks, plane, last=False)
    late_pairs = [column[reach], across[reach], across[reach - 1]]
    return attend(
        doc_lengths, queries, late_pairs, [2 * reach - 1, 2 * reach], [(1, 2), (0, 0)], plane, state=state
    )


def solution(mesh):
    spec = P(("groups", "ctx"), None)
    return jax.shard_map(
        functools.partial(local, mesh.shape["ctx"]),
        mesh=mesh,
        in_specs=(spec, spec, spec, P("groups")),
        out_specs=spec,
        check_vma=False,
    )
```

profile of v0, /device:TPU:1, one launch (start us, length us, event | category | flops | bytes accessed | tf_op | source)
XLA Modules:
  0.0 50.8 jit_solution(16030186072065889176)
XLA Ops:
  0.0 0.9 %constant_dynamic-update-slice_fusion.1 = bf16[128,1024]{1,0:T(8,128)(2,1)S(1)} fusion(bf16[128,512]{1,0:T(8,128)(2,1)} %param.5), kind=kLoop, calls=%fused_computation.1 | loop fusion | bytes 262144
  0.9 0.9 %constant_dynamic-update-slice_fusion.refs_2_ = bf16[128,1024]{1,0:T(8,128)(2,1)S(1)} fusion(bf16[128,1024]{1,0:T(8,128)(2,1)S(1)} %constant_dynamic-update-slice_fusion.1, bf16[128,512]{1,0:T(8,128)(2,1)} %param.6), kind=kLoop, calls=%fused_computation | loop fusion | bytes 262144 | tf_op jit(solution)/shard_map/concatenate | solution.py:140
  1.8 2.2 %collective-permute-start = (bf16[128,1024]{1,0:T(8,128)(2,1)S(1)}, bf16[128,1024]{1,0:T(8,128)(2,1)S(1)}, u32[]{:S(2)}, u32[]{:S(2)}) collective-permute-start(bf16[128,1024]{1,0:T(8,128)(2,1)S(1)} %constant_dynamic-update-slice_fusion.refs_2_), channel_id=1, source_target_pairs={{0,4},{1,5},{2,6},{3,7},{4,8},{5,9},{6,10},{7,11},{8,12},{9,13},{1... | collective-permute-start | bytes 786440 | tf_op jit(solution)/shard_map/ppermute | solution.py:138
  4.0 8.1 %collective-permute-done.refs_4_ = bf16[128,1024]{1,0:T(8,128)(2,1)S(1)} collective-permute-done((bf16[128,1024]{1,0:T(8,128)(2,1)S(1)}, bf16[128,1024]{1,0:T(8,128)(2,1)S(1)}, u32[]{:S(2)}, u32[]{:S(2)}) %collective-permute-start) | collective-permute-done | bytes 262176 | tf_op jit(solution)/shard_map/ppermute | solution.py:138
  12.1 0.0 collective-permute-start.1
  12.1 1.0 %collective-permute-start.9 = (bf16[128,1024]{1,0:T(8,128)(2,1)S(1)}, bf16[128,1024]{1,0:T(8,128)(2,1)S(1)}, u32[]{:S(2)}, u32[]{:S(2)}) collective-permute-start(bf16[128,1024]{1,0:T(8,128)(2,1)S(1)} %constant_dynamic-update-slice_fusion.refs_2_), channel_id=1, source_target_pairs={{0,2},{1,3},{2,0},{3,1},{4,6},{5,7},{6,4},{7,5},{8,10},{9,11},{10,... | collective-permute-start | bytes 786440 | tf_op jit(solution)/shard_map/ppermute | solution.py:135
  13.1 0.5 collective-permute-start.5
  13.5 1.8 %collective-permute-start.7 = (bf16[128,1024]{1,0:T(8,128)(2,1)S(1)}, bf16[128,1024]{1,0:T(8,128)(2,1)S(1)}, u32[]{:S(2)}, u32[]{:S(2)}) collective-permute-start(bf16[128,1024]{1,0:T(8,128)(2,1)S(1)} %constant_dynamic-update-slice_fusion.refs_2_), channel_id=1, source_target_pairs={{0,1},{1,0},{2,3},{3,2},{4,5},{5,4},{6,7},{7,6},{8,9},{9,8},{10,11... | collective-permute-start | bytes 786440 | tf_op jit(solution)/shard_map/ppermute | solution.py:135
  15.3 5.1 %collective-permute-done.1.refs_2_ = bf16[128,1024]{1,0:T(8,128)(2,1)S(1)} collective-permute-done((bf16[128,1024]{1,0:T(8,128)(2,1)S(1)}, bf16[128,1024]{1,0:T(8,128)(2,1)S(1)}, u32[]{:S(2)}, u32[]{:S(2)}) %collective-permute-start.1) | collective-permute-done | bytes 262176 | tf_op jit(solution)/shard_map/ppermute | solution.py:138
  20.4 0.7 %collective-permute-start.3 = (bf16[128,1024]{1,0:T(8,128)(2,1)S(1)}, bf16[128,1024]{1,0:T(8,128)(2,1)S(1)}, u32[]{:S(2)}, u32[]{:S(2)}) collective-permute-start(bf16[128,1024]{1,0:T(8,128)(2,1)S(1)} %collective-permute-done.1.refs_2_), channel_id=1, source_target_pairs={{0,2},{1,3},{2,0},{3,1},{4,6},{5,7},{6,4},{7,5},{8,10},{9,11},{10,... | collective-permute-start | bytes 786440 | tf_op jit(solution)/shard_map/ppermute | solution.py:135
  21.2 2.7 %collective-permute-start.8 = (bf16[128,1024]{1,0:T(8,128)(2,1)S(1)}, bf16[128,1024]{1,0:T(8,128)(2,1)S(1)}, u32[]{:S(2)}, u32[]{:S(2)}) collective-permute-start(bf16[128,1024]{1,0:T(8,128)(2,1)S(1)} %collective-permute-done.refs_4_), channel_id=1, source_target_pairs={{0,1},{1,0},{2,3},{3,2},{4,5},{5,4},{6,7},{7,6},{8,9},{9,8},{10,11... | collective-permute-start | bytes 786440 | tf_op jit(solution)/shard_map/ppermute | solution.py:135
  23.9 0.0 collective-permute-done.9.refs_6_
  23.9 0.0 collective-permute-start.10
  23.9 0.4 collective-permute-done.5.refs_8_.refs_6_
  24.3 3.9 %collective-permute-start.6 = (bf16[128,1024]{1,0:T(8,128)(2,1)S(1)}, bf16[128,1024]{1,0:T(8,128)(2,1)S(1)}, u32[]{:S(2)}, u32[]{:S(2)}) collective-permute-start(bf16[128,1024]{1,0:T(8,128)(2,1)S(1)} %collective-permute-done.5.refs_8_.refs_6_), channel_id=1, source_target_pairs={{0,1},{1,0},{2,3},{3,2},{4,5},{5,4},{6,7},{7,6},{8,9},{9,8},{10,11... | collective-permute-start | bytes 786440 | tf_op jit(solution)/shard_map/ppermute | solution.py:135
  28.2 0.0 collective-permute-done.7.refs_3_
  28.2 0.0 collective-permute-start.2
  28.2 1.7 %collective-permute-done.3.refs_4_ = bf16[128,1024]{1,0:T(8,128)(2,1)S(1)} collective-permute-done((bf16[128,1024]{1,0:T(8,128)(2,1)S(1)}, bf16[128,1024]{1,0:T(8,128)(2,1)S(1)}, u32[]{:S(2)}, u32[]{:S(2)}) %collective-permute-start.3) | collective-permute-done | bytes 262176 | tf_op jit(solution)/shard_map/ppermute | solution.py:135
  29.9 2.1 %collective-permute-start.4 = (bf16[128,1024]{1,0:T(8,128)(2,1)S(1)}, bf16[128,1024]{1,0:T(8,128)(2,1)S(1)}, u32[]{:S(2)}, u32[]{:S(2)}) collective-permute-start(bf16[128,1024]{1,0:T(8,128)(2,1)S(1)} %collective-permute-done.3.refs_4_), channel_id=1, source_target_pairs={{0,1},{1,0},{2,3},{3,2},{4,5},{5,4},{6,7},{7,6},{8,9},{9,8},{10,11... | collective-permute-start | bytes 786440 | tf_op jit(solution)/shard_map/ppermute | solution.py:135
  32.0 0.0 collective-permute-done.8.refs_5_
  32.0 0.0 collective-permute-done.10.refs_7_
  32.0 0.0 collective-permute-done.6.refs_9_.refs_7_
  32.0 0.0 copy-start
  32.1 1.2 %copy-done = bf16[128,4096]{1,0:T(8,128)(2,1)S(1)} copy-done((bf16[128,4096]{1,0:T(8,128)(2,1)S(1)}, bf16[128,4096]{1,0:T(8,128)(2,1)}, u32[]{:S(2)}) %copy-start) | copy-done | bytes 1048600
  33.3 0.0 copy-start.1
  33.3 0.7 %copy-done.1 = s32[16]{0:T(128)S(1)} copy-done((s32[16]{0:T(128)S(1)}, s32[16]{0:T(128)}, u32[]{:S(2)}) %copy-start.1) | copy-done | bytes 88
  33.9 6.0 %shard_map.46 = (f32[128,4096]{1,0:T(8,128)S(1)}, f32[4,128,128]{2,1,0:T(8,128)S(1)}) custom-call(s32[16]{0:T(128)S(1)} %copy-done.1, bf16[128,4096]{1,0:T(8,128)(2,1)S(1)} %copy-done, bf16[128,1024]{1,0:T(8,128)(2,1)S(1)} %constant_dynamic-update-slice_fusion.refs_2_, bf16[128,1024]{1,0:T(8,128)(2,1)S(1)} %collective-permute-done.7.refs_3_, ...), custom_call_target="tpu_custom_call" | custom-call | flops 1610612736 | bytes 3670016 | tf_op jit(solution)/shard_map/pallas_call | solution.py:116
  40.0 0.0 collective-permute-done.2.refs_3_
  40.0 0.0 collective-permute-done.4.refs_5_
  40.0 10.7 %shard_map.47 = bf16[128,4096]{1,0:T(8,128)(2,1)} custom-call(s32[16]{0:T(128)S(1)} %copy-done.1, bf16[128,4096]{1,0:T(8,128)(2,1)S(1)} %copy-done, bf16[128,1024]{1,0:T(8,128)(2,1)S(1)} %collective-permute-done.1.refs_2_, bf16[128,1024]{1,0:T(8,128)(2,1)S(1)} %collective-permute-done.2.refs_3_, bf16[128,1024]{1,0:T(8,128)(2,1)S(1)} %collective-permute-done.3.refs_4_, ...), custom_call_target="tpu_custom_call" | custom-call | flops 1073741824 | bytes 3145728 | tf_op jit(solution)/shard_map/pallas_call | solution.py:116
Async XLA Ops:
  1.8 10.2 %collective-permute-start = (bf16[128,1024]{1,0:T(8,128)(2,1)S(1)}, bf16[128,1024]{1,0:T(8,128)(2,1)S(1)}, u32[]{:S(2)}, u32[]{:S(2)}) collective-permute-start(bf16[128,1024]{1,0:T(8,128)(2,1)S(1)} %constant_dynamic-update-slice_fusion.refs_2_), channel_id=1, source_target_pairs={{0,4},{1,5},{2,6},{3,7},{4,8},{5,9},{6,10},{7,11},{8,12},{9,13},{1... | collective-permute-start | bytes 786440 | tf_op jit(solution)/shard_map/ppermute | solution.py:138
  12.1 8.4 %collective-permute-start.1 = (bf16[128,1024]{1,0:T(8,128)(2,1)S(1)}, bf16[128,1024]{1,0:T(8,128)(2,1)S(1)}, u32[]{:S(2)}, u32[]{:S(2)}) collective-permute-start(bf16[128,1024]{1,0:T(8,128)(2,1)S(1)} %collective-permute-done.refs_4_), channel_id=1, source_target_pairs={{0,4},{1,5},{2,6},{3,7},{4,8},{5,9},{6,10},{7,11},{8,12},{9,13},{1... | collective-permute-start | bytes 786440 | tf_op jit(solution)/shard_map/ppermute | solution.py:138
  12.1 11.8 %collective-permute-start.9 = (bf16[128,1024]{1,0:T(8,128)(2,1)S(1)}, bf16[128,1024]{1,0:T(8,128)(2,1)S(1)}, u32[]{:S(2)}, u32[]{:S(2)}) collective-permute-start(bf16[128,1024]{1,0:T(8,128)(2,1)S(1)} %constant_dynamic-update-slice_fusion.refs_2_), channel_id=1, source_target_pairs={{0,2},{1,3},{2,0},{3,1},{4,6},{5,7},{6,4},{7,5},{8,10},{9,11},{10,... | collective-permute-start | bytes 786440 | tf_op jit(solution)/shard_map/ppermute | solution.py:135
  13.1 11.2 %collective-permute-start.5 = (bf16[128,1024]{1,0:T(8,128)(2,1)S(1)}, bf16[128,1024]{1,0:T(8,128)(2,1)S(1)}, u32[]{:S(2)}, u32[]{:S(2)}) collective-permute-start(bf16[128,1024]{1,0:T(8,128)(2,1)S(1)} %collective-permute-done.refs_4_), channel_id=1, source_target_pairs={{0,2},{1,3},{2,0},{3,1},{4,6},{5,7},{6,4},{7,5},{8,10},{9,11},{10,... | collective-permute-start | bytes 786440 | tf_op jit(solution)/shard_map/ppermute | solution.py:135
  13.5 14.6 %collective-permute-start.7 = (bf16[128,1024]{1,0:T(8,128)(2,1)S(1)}, bf16[128,1024]{1,0:T(8,128)(2,1)S(1)}, u32[]{:S(2)}, u32[]{:S(2)}) collective-permute-start(bf16[128,1024]{1,0:T(8,128)(2,1)S(1)} %constant_dynamic-update-slice_fusion.refs_2_), channel_id=1, source_target_pairs={{0,1},{1,0},{2,3},{3,2},{4,5},{5,4},{6,7},{7,6},{8,9},{9,8},{10,11... | collective-permute-start | bytes 786440 | tf_op jit(solution)/shard_map/ppermute | solution.py:135
  20.4 9.4 %collective-permute-start.3 = (bf16[128,1024]{1,0:T(8,128)(2,1)S(1)}, bf16[128,1024]{1,0:T(8,128)(2,1)S(1)}, u32[]{:S(2)}, u32[]{:S(2)}) collective-permute-start(bf16[128,1024]{1,0:T(8,128)(2,1)S(1)} %collective-permute-done.1.refs_2_), channel_id=1, source_target_pairs={{0,2},{1,3},{2,0},{3,1},{4,6},{5,7},{6,4},{7,5},{8,10},{9,11},{10,... | collective-permute-start | bytes 786440 | tf_op jit(solution)/shard_map/ppermute | solution.py:135
  21.2 10.8 %collective-permute-start.8 = (bf16[128,1024]{1,0:T(8,128)(2,1)S(1)}, bf16[128,1024]{1,0:T(8,128)(2,1)S(1)}, u32[]{:S(2)}, u32[]{:S(2)}) collective-permute-start(bf16[128,1024]{1,0:T(8,128)(2,1)S(1)} %collective-permute-done.refs_4_), channel_id=1, source_target_pairs={{0,1},{1,0},{2,3},{3,2},{4,5},{5,4},{6,7},{7,6},{8,9},{9,8},{10,11... | collective-permute-start | bytes 786440 | tf_op jit(solution)/shard_map/ppermute | solution.py:135
  23.9 8.2 %collective-permute-start.10 = (bf16[128,1024]{1,0:T(8,128)(2,1)S(1)}, bf16[128,1024]{1,0:T(8,128)(2,1)S(1)}, u32[]{:S(2)}, u32[]{:S(2)}) collective-permute-start(bf16[128,1024]{1,0:T(8,128)(2,1)S(1)} %collective-permute-done.9.refs_6_), channel_id=1, source_target_pairs={{0,1},{1,0},{2,3},{3,2},{4,5},{5,4},{6,7},{7,6},{8,9},{9,8},{10,11... | collective-permute-start | bytes 786440 | tf_op jit(solution)/shard_map/ppermute | solution.py:135
  24.3 7.8 %collective-permute-start.6 = (bf16[128,1024]{1,0:T(8,128)(2,1)S(1)}, bf16[128,1024]{1,0:T(8,128)(2,1)S(1)}, u32[]{:S(2)}, u32[]{:S(2)}) collective-permute-start(bf16[128,1024]{1,0:T(8,128)(2,1)S(1)} %collective-permute-done.5.refs_8_.refs_6_), channel_id=1, source_target_pairs={{0,1},{1,0},{2,3},{3,2},{4,5},{5,4},{6,7},{7,6},{8,9},{9,8},{10,11... | collective-permute-start | bytes 786440 | tf_op jit(solution)/shard_map/ppermute | solution.py:135
  28.2 11.8 %collective-permute-start.2 = (bf16[128,1024]{1,0:T(8,128)(2,1)S(1)}, bf16[128,1024]{1,0:T(8,128)(2,1)S(1)}, u32[]{:S(2)}, u32[]{:S(2)}) collective-permute-start(bf16[128,1024]{1,0:T(8,128)(2,1)S(1)} %collective-permute-done.1.refs_2_), channel_id=1, source_target_pairs={{0,1},{1,0},{2,3},{3,2},{4,5},{5,4},{6,7},{7,6},{8,9},{9,8},{10,11... | collective-permute-start | bytes 786440 | tf_op jit(solution)/shard_map/ppermute | solution.py:135
  29.9 10.1 %collective-permute-start.4 = (bf16[128,1024]{1,0:T(8,128)(2,1)S(1)}, bf16[128,1024]{1,0:T(8,128)(2,1)S(1)}, u32[]{:S(2)}, u32[]{:S(2)}) collective-permute-start(bf16[128,1024]{1,0:T(8,128)(2,1)S(1)} %collective-permute-done.3.refs_4_), channel_id=1, source_target_pairs={{0,1},{1,0},{2,3},{3,2},{4,5},{5,4},{6,7},{7,6},{8,9},{9,8},{10,11... | collective-permute-start | bytes 786440 | tf_op jit(solution)/shard_map/ppermute | solution.py:135
  32.0 1.2 %copy-start = (bf16[128,4096]{1,0:T(8,128)(2,1)S(1)}, bf16[128,4096]{1,0:T(8,128)(2,1)}, u32[]{:S(2)}) copy-start(bf16[128,4096]{1,0:T(8,128)(2,1)} %refs_1_.3) | copy-start | bytes 3145732
  33.3 0.7 %copy-start.1 = (s32[16]{0:T(128)S(1)}, s32[16]{0:T(128)}, u32[]{:S(2)}) copy-start(s32[16]{0:T(128)} %refs_0_.3) | copy-start | bytes 196
where the time goes:
time: 50.9 us; the launch traced here: 50.8 us
  Pallas kernels  16.8 us (33%)
  waiting for transfers between devices  15.3 us (30%)
  starting transfers between devices  14.9 us (29%)
  local copies, waits for them, and re-layouts  3.7 us (7%)
    pallas_call x2, Pallas kernels, attend(): pl.pallas_call(functools.partial(attend_kernel, first, last, offsets, pic...  16.8 us
    ppermute x2, waiting for transfers between devices, onward(): return lax.ppermute(x, 'ctx', [(i, (i + plane) % n) for i in range(n)])  13.2 us
    ppermute x9, starting transfers between devices, swap(): return lax.ppermute(x, 'ctx', [(i, i ^ bit) for i in range(n)])  12.7 us
    unnamed x5, local copies, waits for them, and re-layouts  2.79 us
    ppermute x2, starting transfers between devices, onward(): return lax.ppermute(x, 'ctx', [(i, (i + plane) % n) for i in range(n)])  2.18 us
    ppermute x9, waiting for transfers between devices, swap(): return lax.ppermute(x, 'ctx', [(i, i ^ bit) for i in range(n)])  2.12 us
  transfers between devices with their start and end apart: 11, of which 4 were waited for; matrix products, arithmetic and copies ran while one was open for 0% of the time, Pallas kernels for 12%

commit v1 on v0

v1 whole, which is shorter than its diff:
```python
import functools
import math

import jax
import jax.numpy as jnp
from jax import lax
from jax.experimental import pallas as pl
from jax.experimental.pallas import tpu as pltpu
from jax.sharding import PartitionSpec as P

HEADS = 32
KV_HEADS = 4
HEAD_DIM = 128
GROUP = HEADS // KV_HEADS
NEG = -1e30
EXP2_SCALE = math.log2(math.e) / math.sqrt(HEAD_DIM)


def document_starts(doc_ref, position):
    start = jnp.zeros_like(position)
    end = jnp.int32(0)
    for d in range(doc_ref.shape[0]):
        end = end + doc_ref[d]
        start = jnp.where(position >= end, end, start)
    return start


def attend_kernel(first, last, blocks, *refs):
    n_blocks = len(blocks)
    doc_ref, q_ref = refs[:2]
    k_refs, v_refs = refs[2 : 2 + n_blocks], refs[2 + n_blocks : 2 + 2 * n_blocks]
    rest = refs[2 + 2 * n_blocks :]
    if not first:
        acc_in, top_in, total_in = rest[:3]
        rest = rest[3:]
    rows = q_ref.shape[0]
    me = lax.axis_index("ctx")
    plane, y, core = me // 4, me // 2 % 2, me % 2
    lane = lax.broadcasted_iota(jnp.int32, (rows, rows), 1)
    position = me * rows + lax.broadcasted_iota(jnp.int32, (rows, rows), 0)
    start = document_starts(doc_ref, position)
    biases = []
    for back, flip_y, flip_core in blocks:
        block = 4 * (plane - back) + 2 * (1 - y if flip_y else y) + (1 - core if flip_core else core)
        key = block * rows + lane
        biases.append(jnp.where((key >= start) & (key <= position), 0.0, NEG))
    bias = jnp.concatenate(biases, axis=1)
    keys = bias.shape[1]
    ones = jnp.ones((keys, HEAD_DIM), jnp.bfloat16)

    def head_columns(head):
        return pl.ds(pl.multiple_of(head * HEAD_DIM, HEAD_DIM), HEAD_DIM)

    def body(j, carry):
        at = head_columns(j)
        key_tile = jnp.concatenate([r[:, at] for r in k_refs], axis=0)
        value_tile = jnp.concatenate([r[:, at] for r in v_refs], axis=0)
        value_tile = jnp.concatenate([value_tile, ones], axis=1)
        for g in range(GROUP):
            at = head_columns(j * GROUP + g)
            scores = lax.dot_general(
                q_ref[:, at], key_tile, (((1,), (1,)), ((), ())), preferred_element_type=jnp.float32
            )
            scores = scores + bias
            top = jnp.broadcast_to(jnp.max(scores, axis=1, keepdims=True), (rows, HEAD_DIM))
            if not first:
                top_before = top_in[:, at]
                top = jnp.maximum(top, top_before)
            weights = jnp.concatenate(
                [jnp.exp2((scores[:, i : i + HEAD_DIM] - top) * EXP2_SCALE) for i in range(0, keys, HEAD_DIM)], axis=1
            )
            both = jnp.dot(weights.astype(jnp.bfloat16), value_tile, preferred_element_type=jnp.float32)
            acc, total = both[:, :HEAD_DIM], both[:, HEAD_DIM:]
            if not first:
                fade = jnp.exp2((top_before - top) * EXP2_SCALE)
                acc = acc + acc_in[:, at] * fade
                total = total + total_in[:, at] * fade
            if last:
                rest[0][:, at] = (acc / total).astype(jnp.bfloat16)
            else:
                rest[0][:, at] = acc
                rest[1][:, at] = top
                rest[2][:, at] = total
        return carry

    lax.fori_loop(0, KV_HEADS, body, 0)


def attend(doc_lengths, queries, blocks, state=None, last=False):
    rows = queries.shape[0]
    first = state is None
    operands = [doc_lengths, queries] + [kv[0] for kv in blocks.values()] + [kv[1] for kv in blocks.values()]
    operands += list(state or ())
    vmem = pl.BlockSpec(memory_space=pltpu.VMEM)
    in_specs = [pl.BlockSpec(memory_space=pltpu.SMEM)] + [vmem] * (len(operands) - 1)
    if last:
        out_shape, out_specs = jax.ShapeDtypeStruct(queries.shape, jnp.bfloat16), vmem
    else:
        out_shape, out_specs = (jax.ShapeDtypeStruct(queries.shape, jnp.float32),) * 3, (vmem,) * 3
    keys = rows * len(blocks)
    return pl.pallas_call(
        functools.partial(attend_kernel, first, last, tuple(blocks)),
        out_shape=out_shape,
        in_specs=in_specs,
        out_specs=out_specs,
        compiler_params=pltpu.CompilerParams(vmem_limit_bytes=40 * 1024 * 1024),
        cost_estimate=pl.CostEstimate(
            flops=4 * rows * HEADS * HEAD_DIM * keys,
            bytes_accessed=queries.size * 4 + keys * 2 * KV_HEADS * HEAD_DIM * 2,
            transcendentals=rows * HEADS * keys,
        ),
    )(*operands)


def local(n, queries, keys, values, doc_lengths):
    reach = n // 2 // 4

    def swap(kv, bit):
        return tuple(lax.ppermute(x, "ctx", [(i, i ^ bit) for i in range(n)]) for x in kv)

    def onward(kv):
        return tuple(lax.ppermute(x, "ctx", [(i, (i + 4) % n) for i in range(n)]) for x in kv)

    column = [(keys, values)]
    for _ in range(reach):
        column.append(onward(column[-1]))
    across = [swap(kv, 2) for kv in column]

    def with_core(z, y):
        kv = across[z] if y else column[z]
        return {(z, y, 0): kv, (z, y, 1): swap(kv, 1)}

    state = attend(doc_lengths, queries, with_core(0, 0) | with_core(0, 1) | with_core(1, 0))
    for z in range(1, reach):
        state = attend(doc_lengths, queries, with_core(z, 1) | with_core(z + 1, 0), state)
    return attend(doc_lengths, queries, with_core(reach, 1), state, last=True)


def solution(mesh):
    spec = P(("groups", "ctx"), None)
    return jax.shard_map(
        functools.partial(local, mesh.shape["ctx"]),
        mesh=mesh,
        in_specs=(spec, spec, spec, P("groups")),
        out_specs=spec,
        check_vma=False,
    )
```

time: 50.9 us -> 51.6 us (1.014)
  waiting for transfers between devices: 15.3 us -> 8.18 us
  starting transfers between devices: 14.9 us -> 21 us
  local copies, waits for them, and re-layouts: 3.7 us -> 5.03 us
    ppermute x11 -> x22, waiting for transfers between devices: 15.3 us -> 8.18 us  [the longest x4 5.84 us: onward(): lax.ppermute(x, 'ctx', [(i, (i + 4) % n) for i in range(n)])]
    ppermute x11 -> x22, starting transfers between devices: 14.9 us -> 21 us  [the longest x18 16.2 us: swap(): lax.ppermute(x, 'ctx', [(i, i ^ bit) for i in range(n)])]
    unnamed x5 -> x10, local copies, waits for them, and re-layouts: 2.79 us -> 5.03 us
    concatenate x1 -> x0, local copies, waits for them, and re-layouts: 0.92 us -> none  [local(): column = [jnp.concatenate([keys, values], axis=1)]]
    pallas_call x2 -> x3, Pallas kernels: 16.8 us -> 17.1 us  [attend(): pl.pallas_call(functools.partial(attend_kernel, first, last, tuple(blocks...]
  transfers between devices with their start and end apart: 11 -> 22, of which waited for: 4 -> 6; matrix products, arithmetic and copies ran while one was open for 0% -> 0% of each run, Pallas kernels for 12% -> 25%
where the time goes in v1:
time: 51.6 us; the launch traced here: 51.4 us
  starting transfers between devices  21 us (41%)
  Pallas kernels  17.1 us (33%)
  waiting for transfers between devices  8.18 us (16%)
  local copies, waits for them, and re-layouts  5.03 us (10%)
    pallas_call x3, Pallas kernels, attend(): pl.pallas_call(functools.partial(attend_kernel, first, last, tuple(blocks...  17.1 us
    ppermute x18, starting transfers between devices, swap(): lax.ppermute(x, 'ctx', [(i, i ^ bit) for i in range(n)])  16.2 us
    ppermute x4, waiting for transfers between devices, onward(): lax.ppermute(x, 'ctx', [(i, (i + 4) % n) for i in range(n)])  5.84 us
    unnamed x10, local copies, waits for them, and re-layouts  5.03 us
    ppermute x4, starting transfers between devices, onward(): lax.ppermute(x, 'ctx', [(i, (i + 4) % n) for i in range(n)])  4.75 us
    ppermute x18, waiting for transfers between devices, swap(): lax.ppermute(x, 'ctx', [(i, i ^ bit) for i in range(n)])  2.35 us
  transfers between devices with their start and end apart: 22, of which 6 were waited for; matrix products, arithmetic and copies ran while one was open for 0% of the time, Pallas kernels for 25%

profile of v1, /device:TPU:1, one launch (start us, length us, event | category | flops | bytes accessed | tf_op | source)
XLA Modules:
  0.0 51.4 jit_solution(4464729524076897698)
XLA Ops:
  0.0 2.1 %collective-permute-start = (bf16[128,512]{1,0:T(8,128)(2,1)}, bf16[128,512]{1,0:T(8,128)(2,1)S(1)}, u32[]{:S(2)}, u32[]{:S(2)}) collective-permute-start(bf16[128,512]{1,0:T(8,128)(2,1)} %refs_2_.1), channel_id=1, source_target_pairs={{0,4},{1,5},{2,6},{3,7},{4,8},{5,9},{6,10},{7,11},{8,12},{9,13},{1... | collective-permute-start | bytes 393224 | tf_op jit(solution)/shard_map/ppermute | solution.py:122
  2.1 1.3 %collective-permute-start.4 = (bf16[128,512]{1,0:T(8,128)(2,1)}, bf16[128,512]{1,0:T(8,128)(2,1)S(1)}, u32[]{:S(2)}, u32[]{:S(2)}) collective-permute-start(bf16[128,512]{1,0:T(8,128)(2,1)} %refs_8_.1), channel_id=1, source_target_pairs={{0,4},{1,5},{2,6},{3,7},{4,8},{5,9},{6,10},{7,11},{8,12},{9,13},{1... | collective-permute-start | bytes 393224 | tf_op jit(solution)/shard_map/ppermute | solution.py:122
  3.4 1.2 %collective-permute-start.15 = (bf16[128,512]{1,0:T(8,128)(2,1)}, bf16[128,512]{1,0:T(8,128)(2,1)S(1)}, u32[]{:S(2)}, u32[]{:S(2)}) collective-permute-start(bf16[128,512]{1,0:T(8,128)(2,1)} %refs_2_.1), channel_id=1, source_target_pairs={{0,2},{1,3},{2,0},{3,1},{4,6},{5,7},{6,4},{7,5},{8,10},{9,11},{10,... | collective-permute-start | bytes 393224 | tf_op jit(solution)/shard_map/ppermute | solution.py:119
  4.7 0.2 collective-permute-start.19
  4.9 1.8 %collective-permute-start.14 = (bf16[128,512]{1,0:T(8,128)(2,1)}, bf16[128,512]{1,0:T(8,128)(2,1)S(1)}, u32[]{:S(2)}, u32[]{:S(2)}) collective-permute-start(bf16[128,512]{1,0:T(8,128)(2,1)} %refs_2_.1), channel_id=1, source_target_pairs={{0,1},{1,0},{2,3},{3,2},{4,5},{5,4},{6,7},{7,6},{8,9},{9,8},{10,11... | collective-permute-start | bytes 393224 | tf_op jit(solution)/shard_map/ppermute | solution.py:119
  6.7 0.9 %collective-permute-done.refs_6_ = bf16[128,512]{1,0:T(8,128)(2,1)S(1)} collective-permute-done((bf16[128,512]{1,0:T(8,128)(2,1)}, bf16[128,512]{1,0:T(8,128)(2,1)S(1)}, u32[]{:S(2)}, u32[]{:S(2)}) %collective-permute-start) | collective-permute-done | bytes 131104 | tf_op jit(solution)/shard_map/ppermute | solution.py:122
  7.6 2.1 %collective-permute-start.18 = (bf16[128,512]{1,0:T(8,128)(2,1)}, bf16[128,512]{1,0:T(8,128)(2,1)S(1)}, u32[]{:S(2)}, u32[]{:S(2)}) collective-permute-start(bf16[128,512]{1,0:T(8,128)(2,1)} %refs_8_.1), channel_id=1, source_target_pairs={{0,1},{1,0},{2,3},{3,2},{4,5},{5,4},{6,7},{7,6},{8,9},{9,8},{10,11... | collective-permute-start | bytes 393224 | tf_op jit(solution)/shard_map/ppermute | solution.py:119
  9.6 0.8 %collective-permute-done.4.refs_12_ = bf16[128,512]{1,0:T(8,128)(2,1)S(1)} collective-permute-done((bf16[128,512]{1,0:T(8,128)(2,1)}, bf16[128,512]{1,0:T(8,128)(2,1)S(1)}, u32[]{:S(2)}, u32[]{:S(2)}) %collective-permute-start.4) | collective-permute-done | bytes 131104 | tf_op jit(solution)/shard_map/ppermute | solution.py:122
  10.4 1.2 %collective-permute-start.17 = (bf16[128,512]{1,0:T(8,128)(2,1)S(1)}, bf16[128,512]{1,0:T(8,128)(2,1)S(1)}, u32[]{:S(2)}, u32[]{:S(2)}) collective-permute-start(bf16[128,512]{1,0:T(8,128)(2,1)S(1)} %collective-permute-done.refs_6_), channel_id=1, source_target_pairs={{0,1},{1,0},{2,3},{3,2},{4,5},{5,4},{6,7},{7,6},{8,9},{9,8},{10,11... | collective-permute-start | bytes 393224 | tf_op jit(solution)/shard_map/ppermute | solution.py:119
  11.6 0.0 collective-permute-done.15.refs_4_
  11.6 0.0 collective-permute-start.21
  11.6 0.0 collective-permute-done.19.refs_10_
  11.6 0.7 %collective-permute-start.16 = (bf16[128,512]{1,0:T(8,128)(2,1)S(1)}, bf16[128,512]{1,0:T(8,128)(2,1)S(1)}, u32[]{:S(2)}, u32[]{:S(2)}) collective-permute-start(bf16[128,512]{1,0:T(8,128)(2,1)S(1)} %collective-permute-done.15.refs_4_), channel_id=1, source_target_pairs={{0,1},{1,0},{2,3},{3,2},{4,5},{5,4},{6,7},{7,6},{8,9},{9,8},{10,11... | collective-permute-start | bytes 393224 | tf_op jit(solution)/shard_map/ppermute | solution.py:119
  12.4 0.0 collective-permute-done.14.refs_3_
  12.4 1.3 %collective-permute-start.1 = (bf16[128,512]{1,0:T(8,128)(2,1)S(1)}, bf16[128,512]{1,0:T(8,128)(2,1)S(1)}, u32[]{:S(2)}, u32[]{:S(2)}) collective-permute-start(bf16[128,512]{1,0:T(8,128)(2,1)S(1)} %collective-permute-done.refs_6_), channel_id=1, source_target_pairs={{0,4},{1,5},{2,6},{3,7},{4,8},{5,9},{6,10},{7,11},{8,12},{9,13},{1... | collective-permute-start | bytes 393224 | tf_op jit(solution)/shard_map/ppermute | solution.py:122
  13.7 0.0 collective-permute-done.18.refs_9_
  13.7 0.3 collective-permute-start.20
  13.9 0.0 collective-permute-done.17.refs_7_
  13.9 0.0 collective-permute-start.5
  14.0 0.0 collective-permute-done.21.refs_13_
  14.0 1.3 %collective-permute-start.11 = (bf16[128,512]{1,0:T(8,128)(2,1)S(1)}, bf16[128,512]{1,0:T(8,128)(2,1)S(1)}, u32[]{:S(2)}, u32[]{:S(2)}) collective-permute-start(bf16[128,512]{1,0:T(8,128)(2,1)S(1)} %collective-permute-done.4.refs_12_), channel_id=1, source_target_pairs={{0,2},{1,3},{2,0},{3,1},{4,6},{5,7},{6,4},{7,5},{8,10},{9,11},{10,... | collective-permute-start | bytes 393224 | tf_op jit(solution)/shard_map/ppermute | solution.py:119
  15.3 0.0 collective-permute-done.16.refs_5_
  15.3 0.2 collective-permute-start.8
  15.5 3.8 %collective-permute-done.1.refs_4_ = bf16[128,512]{1,0:T(8,128)(2,1)S(1)} collective-permute-done((bf16[128,512]{1,0:T(8,128)(2,1)S(1)}, bf16[128,512]{1,0:T(8,128)(2,1)S(1)}, u32[]{:S(2)}, u32[]{:S(2)}) %collective-permute-start.1) | collective-permute-done | bytes 131104 | tf_op jit(solution)/shard_map/ppermute | solution.py:122
  19.3 1.2 %collective-permute-start.10 = (bf16[128,512]{1,0:T(8,128)(2,1)S(1)}, bf16[128,512]{1,0:T(8,128)(2,1)S(1)}, u32[]{:S(2)}, u32[]{:S(2)}) collective-permute-start(bf16[128,512]{1,0:T(8,128)(2,1)S(1)} %collective-permute-done.1.refs_4_), channel_id=1, source_target_pairs={{0,1},{1,0},{2,3},{3,2},{4,5},{5,4},{6,7},{7,6},{8,9},{9,8},{10,11... | collective-permute-start | bytes 393224 | tf_op jit(solution)/shard_map/ppermute | solution.py:119
  20.5 0.0 collective-permute-done.20.refs_11_
  20.5 1.2 %collective-permute-start.2 = (bf16[128,512]{1,0:T(8,128)(2,1)S(1)}, bf16[128,512]{1,0:T(8,128)(2,1)S(1)}, u32[]{:S(2)}, u32[]{:S(2)}) collective-permute-start(bf16[128,512]{1,0:T(8,128)(2,1)S(1)} %collective-permute-done.1.refs_4_), channel_id=1, source_target_pairs={{0,2},{1,3},{2,0},{3,1},{4,6},{5,7},{6,4},{7,5},{8,10},{9,11},{10,... | collective-permute-start | bytes 393224 | tf_op jit(solution)/shard_map/ppermute | solution.py:119
  21.7 0.4 collective-permute-done.5.refs_8_
  22.1 1.2 %collective-permute-start.6 = (bf16[128,512]{1,0:T(8,128)(2,1)S(1)}, bf16[128,512]{1,0:T(8,128)(2,1)S(1)}, u32[]{:S(2)}, u32[]{:S(2)}) collective-permute-start(bf16[128,512]{1,0:T(8,128)(2,1)S(1)} %collective-permute-done.5.refs_8_), channel_id=1, source_target_pairs={{0,2},{1,3},{2,0},{3,1},{4,6},{5,7},{6,4},{7,5},{8,10},{9,11},{10,... | collective-permute-start | bytes 393224 | tf_op jit(solution)/shard_map/ppermute | solution.py:119
  23.3 0.0 collective-permute-done.11.refs_6_
  23.3 1.1 %collective-permute-start.13 = (bf16[128,512]{1,0:T(8,128)(2,1)S(1)}, bf16[128,512]{1,0:T(8,128)(2,1)S(1)}, u32[]{:S(2)}, u32[]{:S(2)}) collective-permute-start(bf16[128,512]{1,0:T(8,128)(2,1)S(1)} %collective-permute-done.5.refs_8_), channel_id=1, source_target_pairs={{0,1},{1,0},{2,3},{3,2},{4,5},{5,4},{6,7},{7,6},{8,9},{9,8},{10,11... | collective-permute-start | bytes 393224 | tf_op jit(solution)/shard_map/ppermute | solution.py:119
  24.4 0.0 collective-permute-done.8.refs_2_
  24.4 0.1 collective-permute-start.12
  24.5 0.0 collective-permute-done.10.refs_5_
  24.5 0.4 collective-permute-start.9
  24.9 0.7 %collective-permute-done.2.refs_2_ = bf16[128,512]{1,0:T(8,128)(2,1)S(1)} collective-permute-done((bf16[128,512]{1,0:T(8,128)(2,1)S(1)}, bf16[128,512]{1,0:T(8,128)(2,1)S(1)}, u32[]{:S(2)}, u32[]{:S(2)}) %collective-permute-start.2) | collective-permute-done | bytes 131104 | tf_op jit(solution)/shard_map/ppermute | solution.py:119
  25.6 1.2 %collective-permute-start.3 = (bf16[128,512]{1,0:T(8,128)(2,1)S(1)}, bf16[128,512]{1,0:T(8,128)(2,1)S(1)}, u32[]{:S(2)}, u32[]{:S(2)}) collective-permute-start(bf16[128,512]{1,0:T(8,128)(2,1)S(1)} %collective-permute-done.2.refs_2_), channel_id=1, source_target_pairs={{0,1},{1,0},{2,3},{3,2},{4,5},{5,4},{6,7},{7,6},{8,9},{9,8},{10,11... | collective-permute-start | bytes 393224 | tf_op jit(solution)/shard_map/ppermute | solution.py:119
  26.8 1.6 %collective-permute-done.6.refs_4_ = bf16[128,512]{1,0:T(8,128)(2,1)S(1)} collective-permute-done((bf16[128,512]{1,0:T(8,128)(2,1)S(1)}, bf16[128,512]{1,0:T(8,128)(2,1)S(1)}, u32[]{:S(2)}, u32[]{:S(2)}) %collective-permute-start.6) | collective-permute-done | bytes 131104 | tf_op jit(solution)/shard_map/ppermute | solution.py:119
  28.4 0.8 %collective-permute-start.7 = (bf16[128,512]{1,0:T(8,128)(2,1)S(1)}, bf16[128,512]{1,0:T(8,128)(2,1)S(1)}, u32[]{:S(2)}, u32[]{:S(2)}) collective-permute-start(bf16[128,512]{1,0:T(8,128)(2,1)S(1)} %collective-permute-done.6.refs_4_), channel_id=1, source_target_pairs={{0,1},{1,0},{2,3},{3,2},{4,5},{5,4},{6,7},{7,6},{8,9},{9,8},{10,11... | collective-permute-start | bytes 393224 | tf_op jit(solution)/shard_map/ppermute | solution.py:119
  29.2 0.0 copy-start
  29.2 1.2 %copy-done = bf16[128,4096]{1,0:T(8,128)(2,1)S(1)} copy-done((bf16[128,4096]{1,0:T(8,128)(2,1)S(1)}, bf16[128,4096]{1,0:T(8,128)(2,1)}, u32[]{:S(2)}) %copy-start) | copy-done | bytes 1048600
  30.4 0.0 copy-start.2
  30.4 0.7 %copy-done.2 = s32[16]{0:T(128)S(1)} copy-done((s32[16]{0:T(128)S(1)}, s32[16]{0:T(128)}, u32[]{:S(2)}) %copy-start.2) | copy-done | bytes 88
  31.1 0.0 copy-start.3
  31.1 0.9 %copy-done.3 = bf16[128,512]{1,0:T(8,128)(2,1)S(1)} copy-done((bf16[128,512]{1,0:T(8,128)(2,1)S(1)}, bf16[128,512]{1,0:T(8,128)(2,1)}, u32[]{:S(2)}) %copy-start.3) | copy-done | bytes 131096
  32.0 0.0 copy-start.4
  32.0 0.9 %copy-done.4 = bf16[128,512]{1,0:T(8,128)(2,1)S(1)} copy-done((bf16[128,512]{1,0:T(8,128)(2,1)S(1)}, bf16[128,512]{1,0:T(8,128)(2,1)}, u32[]{:S(2)}) %copy-start.4) | copy-done | bytes 131096
  32.9 6.5 %shard_map.46 = (f32[128,4096]{1,0:T(8,128)S(1)}, f32[128,4096]{1,0:T(8,128)S(1)}, f32[128,4096]{1,0:T(8,128)S(1)}) custom-call(s32[16]{0:T(128)S(1)} %copy-done.2, bf16[128,4096]{1,0:T(8,128)(2,1)S(1)} %copy-done, bf16[128,512]{1,0:T(8,128)(2,1)S(1)} %copy-done.3, bf16[128,512]{1,0:T(8,128)(2,1)S(1)} %collective-permute-done.14.refs_3_, ...), custom_call_target="tpu_custom_call" | custom-call | flops 1610612736 | bytes 3670016 | tf_op jit(solution)/shard_map/pallas_call | solution.py:101
  39.4 0.0 copy-start.1
  39.4 1.3 %copy-done.1 = f32[128,4096]{1,0:T(8,128)} copy-done((f32[128,4096]{1,0:T(8,128)}, f32[128,4096]{1,0:T(8,128)S(1)}, u32[]{:S(2)}) %copy-start.1) | copy-done | bytes 2097176
  40.7 0.0 collective-permute-done.13.refs_9_
  40.7 0.0 collective-permute-done.12.refs_7_
  40.7 0.0 collective-permute-done.9.refs_3_
  40.7 6.2 %shard_map.47 = (f32[128,4096]{1,0:T(8,128)S(1)}, f32[128,4096]{1,0:T(8,128)S(1)}, f32[128,4096]{1,0:T(8,128)S(1)}) custom-call(s32[16]{0:T(128)S(1)} %copy-done.2, bf16[128,4096]{1,0:T(8,128)(2,1)S(1)} %copy-done, bf16[128,512]{1,0:T(8,128)(2,1)S(1)} %collective-permute-done.8.refs_2_, bf16[128,512]{1,0:T(8,128)(2,1)S(1)} %collective-permute-done.9.refs_3_, ...), custom_call_target="tpu_custom_call" | custom-call | flops 1073741824 | bytes 3145728 | tf_op jit(solution)/shard_map/pallas_call | solution.py:101
  46.9 0.0 collective-permute-done.3.refs_3_
  46.9 0.0 collective-permute-done.7.refs_5_
  46.9 4.4 %shard_map.48 = bf16[128,4096]{1,0:T(8,128)(2,1)} custom-call(s32[16]{0:T(128)S(1)} %copy-done.2, bf16[128,4096]{1,0:T(8,128)(2,1)S(1)} %copy-done, bf16[128,512]{1,0:T(8,128)(2,1)S(1)} %collective-permute-done.2.refs_2_, bf16[128,512]{1,0:T(8,128)(2,1)S(1)} %collective-permute-done.3.refs_3_, bf16[128,512]{1,0:T(8,128)(2,1)S(1)} %collective-permute-done.6.refs_4_, ...), custom_call_target="tpu_custom_call" | custom-call | flops 536870912 | bytes 2621440 | tf_op jit(solution)/shard_map/pallas_call | solution.py:101
Async XLA Ops:
  0.0 7.6 %collective-permute-start = (bf16[128,512]{1,0:T(8,128)(2,1)}, bf16[128,512]{1,0:T(8,128)(2,1)S(1)}, u32[]{:S(2)}, u32[]{:S(2)}) collective-permute-start(bf16[128,512]{1,0:T(8,128)(2,1)} %refs_2_.1), channel_id=1, source_target_pairs={{0,4},{1,5},{2,6},{3,7},{4,8},{5,9},{6,10},{7,11},{8,12},{9,13},{1... | collective-permute-start | bytes 393224 | tf_op jit(solution)/shard_map/ppermute | solution.py:122
  2.1 8.3 %collective-permute-start.4 = (bf16[128,512]{1,0:T(8,128)(2,1)}, bf16[128,512]{1,0:T(8,128)(2,1)S(1)}, u32[]{:S(2)}, u32[]{:S(2)}) collective-permute-start(bf16[128,512]{1,0:T(8,128)(2,1)} %refs_8_.1), channel_id=1, source_target_pairs={{0,4},{1,5},{2,6},{3,7},{4,8},{5,9},{6,10},{7,11},{8,12},{9,13},{1... | collective-permute-start | bytes 393224 | tf_op jit(solution)/shard_map/ppermute | solution.py:122
  3.4 8.2 %collective-permute-start.15 = (bf16[128,512]{1,0:T(8,128)(2,1)}, bf16[128,512]{1,0:T(8,128)(2,1)S(1)}, u32[]{:S(2)}, u32[]{:S(2)}) collective-permute-start(bf16[128,512]{1,0:T(8,128)(2,1)} %refs_2_.1), channel_id=1, source_target_pairs={{0,2},{1,3},{2,0},{3,1},{4,6},{5,7},{6,4},{7,5},{8,10},{9,11},{10,... | collective-permute-start | bytes 393224 | tf_op jit(solution)/shard_map/ppermute | solution.py:119
  4.7 7.0 %collective-permute-start.19 = (bf16[128,512]{1,0:T(8,128)(2,1)}, bf16[128,512]{1,0:T(8,128)(2,1)S(1)}, u32[]{:S(2)}, u32[]{:S(2)}) collective-permute-start(bf16[128,512]{1,0:T(8,128)(2,1)} %refs_8_.1), channel_id=1, source_target_pairs={{0,2},{1,3},{2,0},{3,1},{4,6},{5,7},{6,4},{7,5},{8,10},{9,11},{10,... | collective-permute-start | bytes 393224 | tf_op jit(solution)/shard_map/ppermute | solution.py:119
  4.9 7.5 %collective-permute-start.14 = (bf16[128,512]{1,0:T(8,128)(2,1)}, bf16[128,512]{1,0:T(8,128)(2,1)S(1)}, u32[]{:S(2)}, u32[]{:S(2)}) collective-permute-start(bf16[128,512]{1,0:T(8,128)(2,1)} %refs_2_.1), channel_id=1, source_target_pairs={{0,1},{1,0},{2,3},{3,2},{4,5},{5,4},{6,7},{7,6},{8,9},{9,8},{10,11... | collective-permute-start | bytes 393224 | tf_op jit(solution)/shard_map/ppermute | solution.py:119
  7.6 6.1 %collective-permute-start.18 = (bf16[128,512]{1,0:T(8,128)(2,1)}, bf16[128,512]{1,0:T(8,128)(2,1)S(1)}, u32[]{:S(2)}, u32[]{:S(2)}) collective-permute-start(bf16[128,512]{1,0:T(8,128)(2,1)} %refs_8_.1), channel_id=1, source_target_pairs={{0,1},{1,0},{2,3},{3,2},{4,5},{5,4},{6,7},{7,6},{8,9},{9,8},{10,11... | collective-permute-start | bytes 393224 | tf_op jit(solution)/shard_map/ppermute | solution.py:119
  10.4 3.6 %collective-permute-start.17 = (bf16[128,512]{1,0:T(8,128)(2,1)S(1)}, bf16[128,512]{1,0:T(8,128)(2,1)S(1)}, u32[]{:S(2)}, u32[]{:S(2)}) collective-permute-start(bf16[128,512]{1,0:T(8,128)(2,1)S(1)} %collective-permute-done.refs_6_), channel_id=1, source_target_pairs={{0,1},{1,0},{2,3},{3,2},{4,5},{5,4},{6,7},{7,6},{8,9},{9,8},{10,11... | collective-permute-start | bytes 393224 | tf_op jit(solution)/shard_map/ppermute | solution.py:119
  11.6 2.4 %collective-permute-start.21 = (bf16[128,512]{1,0:T(8,128)(2,1)S(1)}, bf16[128,512]{1,0:T(8,128)(2,1)S(1)}, u32[]{:S(2)}, u32[]{:S(2)}) collective-permute-start(bf16[128,512]{1,0:T(8,128)(2,1)S(1)} %collective-permute-done.4.refs_12_), channel_id=1, source_target_pairs={{0,1},{1,0},{2,3},{3,2},{4,5},{5,4},{6,7},{7,6},{8,9},{9,8},{10,11... | collective-permute-start | bytes 393224 | tf_op jit(solution)/shard_map/ppermute | solution.py:119
  11.6 3.6 %collective-permute-start.16 = (bf16[128,512]{1,0:T(8,128)(2,1)S(1)}, bf16[128,512]{1,0:T(8,128)(2,1)S(1)}, u32[]{:S(2)}, u32[]{:S(2)}) collective-permute-start(bf16[128,512]{1,0:T(8,128)(2,1)S(1)} %collective-permute-done.15.refs_4_), channel_id=1, source_target_pairs={{0,1},{1,0},{2,3},{3,2},{4,5},{5,4},{6,7},{7,6},{8,9},{9,8},{10,11... | collective-permute-start | bytes 393224 | tf_op jit(solution)/shard_map/ppermute | solution.py:119
  12.4 6.9 %collective-permute-start.1 = (bf16[128,512]{1,0:T(8,128)(2,1)S(1)}, bf16[128,512]{1,0:T(8,128)(2,1)S(1)}, u32[]{:S(2)}, u32[]{:S(2)}) collective-permute-start(bf16[128,512]{1,0:T(8,128)(2,1)S(1)} %collective-permute-done.refs_6_), channel_id=1, source_target_pairs={{0,4},{1,5},{2,6},{3,7},{4,8},{5,9},{6,10},{7,11},{8,12},{9,13},{1... | collective-permute-start | bytes 393224 | tf_op jit(solution)/shard_map/ppermute | solution.py:122
  13.7 6.8 %collective-permute-start.20 = (bf16[128,512]{1,0:T(8,128)(2,1)S(1)}, bf16[128,512]{1,0:T(8,128)(2,1)S(1)}, u32[]{:S(2)}, u32[]{:S(2)}) collective-permute-start(bf16[128,512]{1,0:T(8,128)(2,1)S(1)} %collective-permute-done.19.refs_10_), channel_id=1, source_target_pairs={{0,1},{1,0},{2,3},{3,2},{4,5},{5,4},{6,7},{7,6},{8,9},{9,8},{10,11... | collective-permute-start | bytes 393224 | tf_op jit(solution)/shard_map/ppermute | solution.py:119
  13.9 8.1 %collective-permute-start.5 = (bf16[128,512]{1,0:T(8,128)(2,1)S(1)}, bf16[128,512]{1,0:T(8,128)(2,1)S(1)}, u32[]{:S(2)}, u32[]{:S(2)}) collective-permute-start(bf16[128,512]{1,0:T(8,128)(2,1)S(1)} %collective-permute-done.4.refs_12_), channel_id=1, source_target_pairs={{0,4},{1,5},{2,6},{3,7},{4,8},{5,9},{6,10},{7,11},{8,12},{9,13},{1... | collective-permute-start | bytes 393224 | tf_op jit(solution)/shard_map/ppermute | solution.py:122
  14.0 9.4 %collective-permute-start.11 = (bf16[128,512]{1,0:T(8,128)(2,1)S(1)}, bf16[128,512]{1,0:T(8,128)(2,1)S(1)}, u32[]{:S(2)}, u32[]{:S(2)}) collective-permute-start(bf16[128,512]{1,0:T(8,128)(2,1)S(1)} %collective-permute-done.4.refs_12_), channel_id=1, source_target_pairs={{0,2},{1,3},{2,0},{3,1},{4,6},{5,7},{6,4},{7,5},{8,10},{9,11},{10,... | collective-permute-start | bytes 393224 | tf_op jit(solution)/shard_map/ppermute | solution.py:119
  15.3 9.1 %collective-permute-start.8 = (bf16[128,512]{1,0:T(8,128)(2,1)S(1)}, bf16[128,512]{1,0:T(8,128)(2,1)S(1)}, u32[]{:S(2)}, u32[]{:S(2)}) collective-permute-start(bf16[128,512]{1,0:T(8,128)(2,1)S(1)} %collective-permute-done.refs_6_), channel_id=1, source_target_pairs={{0,2},{1,3},{2,0},{3,1},{4,6},{5,7},{6,4},{7,5},{8,10},{9,11},{10,... | collective-permute-start | bytes 393224 | tf_op jit(solution)/shard_map/ppermute | solution.py:119
  19.3 5.2 %collective-permute-start.10 = (bf16[128,512]{1,0:T(8,128)(2,1)S(1)}, bf16[128,512]{1,0:T(8,128)(2,1)S(1)}, u32[]{:S(2)}, u32[]{:S(2)}) collective-permute-start(bf16[128,512]{1,0:T(8,128)(2,1)S(1)} %collective-permute-done.1.refs_4_), channel_id=1, source_target_pairs={{0,1},{1,0},{2,3},{3,2},{4,5},{5,4},{6,7},{7,6},{8,9},{9,8},{10,11... | collective-permute-start | bytes 393224 | tf_op jit(solution)/shard_map/ppermute | solution.py:119
  20.5 5.1 %collective-permute-start.2 = (bf16[128,512]{1,0:T(8,128)(2,1)S(1)}, bf16[128,512]{1,0:T(8,128)(2,1)S(1)}, u32[]{:S(2)}, u32[]{:S(2)}) collective-permute-start(bf16[128,512]{1,0:T(8,128)(2,1)S(1)} %collective-permute-done.1.refs_4_), channel_id=1, source_target_pairs={{0,2},{1,3},{2,0},{3,1},{4,6},{5,7},{6,4},{7,5},{8,10},{9,11},{10,... | collective-permute-start | bytes 393224 | tf_op jit(solution)/shard_map/ppermute | solution.py:119
  22.1 6.3 %collective-permute-start.6 = (bf16[128,512]{1,0:T(8,128)(2,1)S(1)}, bf16[128,512]{1,0:T(8,128)(2,1)S(1)}, u32[]{:S(2)}, u32[]{:S(2)}) collective-permute-start(bf16[128,512]{1,0:T(8,128)(2,1)S(1)} %collective-permute-done.5.refs_8_), channel_id=1, source_target_pairs={{0,2},{1,3},{2,0},{3,1},{4,6},{5,7},{6,4},{7,5},{8,10},{9,11},{10,... | collective-permute-start | bytes 393224 | tf_op jit(solution)/shard_map/ppermute | solution.py:119
  23.3 17.4 %collective-permute-start.13 = (bf16[128,512]{1,0:T(8,128)(2,1)S(1)}, bf16[128,512]{1,0:T(8,128)(2,1)S(1)}, u32[]{:S(2)}, u32[]{:S(2)}) collective-permute-start(bf16[128,512]{1,0:T(8,128)(2,1)S(1)} %collective-permute-done.5.refs_8_), channel_id=1, source_target_pairs={{0,1},{1,0},{2,3},{3,2},{4,5},{5,4},{6,7},{7,6},{8,9},{9,8},{10,11... | collective-permute-start | bytes 393224 | tf_op jit(solution)/shard_map/ppermute | solution.py:119
  24.4 16.3 %collective-permute-start.12 = (bf16[128,512]{1,0:T(8,128)(2,1)S(1)}, bf16[128,512]{1,0:T(8,128)(2,1)S(1)}, u32[]{:S(2)}, u32[]{:S(2)}) collective-permute-start(bf16[128,512]{1,0:T(8,128)(2,1)S(1)} %collective-permute-done.11.refs_6_), channel_id=1, source_target_pairs={{0,1},{1,0},{2,3},{3,2},{4,5},{5,4},{6,7},{7,6},{8,9},{9,8},{10,11... | collective-permute-start | bytes 393224 | tf_op jit(solution)/shard_map/ppermute | solution.py:119
  24.5 16.3 %collective-permute-start.9 = (bf16[128,512]{1,0:T(8,128)(2,1)S(1)}, bf16[128,512]{1,0:T(8,128)(2,1)S(1)}, u32[]{:S(2)}, u32[]{:S(2)}) collective-permute-start(bf16[128,512]{1,0:T(8,128)(2,1)S(1)} %collective-permute-done.8.refs_2_), channel_id=1, source_target_pairs={{0,1},{1,0},{2,3},{3,2},{4,5},{5,4},{6,7},{7,6},{8,9},{9,8},{10,11... | collective-permute-start | bytes 393224 | tf_op jit(solution)/shard_map/ppermute | solution.py:119
  25.6 21.3 %collective-permute-start.3 = (bf16[128,512]{1,0:T(8,128)(2,1)S(1)}, bf16[128,512]{1,0:T(8,128)(2,1)S(1)}, u32[]{:S(2)}, u32[]{:S(2)}) collective-permute-start(bf16[128,512]{1,0:T(8,128)(2,1)S(1)} %collective-permute-done.2.refs_2_), channel_id=1, source_target_pairs={{0,1},{1,0},{2,3},{3,2},{4,5},{5,4},{6,7},{7,6},{8,9},{9,8},{10,11... | collective-permute-start | bytes 393224 | tf_op jit(solution)/shard_map/ppermute | solution.py:119
  28.4 18.5 %collective-permute-start.7 = (bf16[128,512]{1,0:T(8,128)(2,1)S(1)}, bf16[128,512]{1,0:T(8,128)(2,1)S(1)}, u32[]{:S(2)}, u32[]{:S(2)}) collective-permute-start(bf16[128,512]{1,0:T(8,128)(2,1)S(1)} %collective-permute-done.6.refs_4_), channel_id=1, source_target_pairs={{0,1},{1,0},{2,3},{3,2},{4,5},{5,4},{6,7},{7,6},{8,9},{9,8},{10,11... | collective-permute-start | bytes 393224 | tf_op jit(solution)/shard_map/ppermute | solution.py:119
  29.2 1.2 %copy-start = (bf16[128,4096]{1,0:T(8,128)(2,1)S(1)}, bf16[128,4096]{1,0:T(8,128)(2,1)}, u32[]{:S(2)}) copy-start(bf16[128,4096]{1,0:T(8,128)(2,1)} %refs_1_.5) | copy-start | bytes 3145732
  30.4 0.7 %copy-start.2 = (s32[16]{0:T(128)S(1)}, s32[16]{0:T(128)}, u32[]{:S(2)}) copy-start(s32[16]{0:T(128)} %refs_0_.5) | copy-start | bytes 196
  31.1 0.9 %copy-start.3 = (bf16[128,512]{1,0:T(8,128)(2,1)S(1)}, bf16[128,512]{1,0:T(8,128)(2,1)}, u32[]{:S(2)}) copy-start(bf16[128,512]{1,0:T(8,128)(2,1)} %refs_2_.1) | copy-start | bytes 393220
  32.0 0.9 %copy-start.4 = (bf16[128,512]{1,0:T(8,128)(2,1)S(1)}, bf16[128,512]{1,0:T(8,128)(2,1)}, u32[]{:S(2)}) copy-start(bf16[128,512]{1,0:T(8,128)(2,1)} %refs_8_.1) | copy-start | bytes 393220
  39.4 1.3 %copy-start.1 = (f32[128,4096]{1,0:T(8,128)}, f32[128,4096]{1,0:T(8,128)S(1)}, u32[]{:S(2)}) copy-start(f32[128,4096]{1,0:T(8,128)S(1)} %get-tuple-element.13.refs_12_) | copy-start | bytes 6291460

commit v2 on v1

v2 whole, which is shorter than its diff:
```python
import functools
import math

import jax
import jax.numpy as jnp
from jax import lax
from jax.experimental import pallas as pl
from jax.experimental.pallas import tpu as pltpu
from jax.sharding import PartitionSpec as P

HEADS = 32
KV_HEADS = 4
HEAD_DIM = 128
GROUP = HEADS // KV_HEADS
NEG = -1e30
EXP2_SCALE = math.log2(math.e) / math.sqrt(HEAD_DIM)
VMEM = pl.BlockSpec(memory_space=pltpu.VMEM)
HBM = pl.BlockSpec(memory_space=pltpu.HBM)


def head_columns(head, count=1):
    return pl.ds(head * HEAD_DIM, count * HEAD_DIM)


def document_starts(doc_ref, position):
    start = jnp.zeros_like(position)
    end = jnp.int32(0)
    for d in range(doc_ref.shape[0]):
        end = end + doc_ref[d]
        start = jnp.where(position >= end, end, start)
    return start


def place():
    me = lax.axis_index("ctx")
    return me // 4, me // 2 % 2, me % 2


def update_heads(j, q_ref, key_tile, value_tile, bias, state, emit):
    rows, keys = bias.shape
    value_tile = jnp.concatenate([value_tile, jnp.ones((keys, HEAD_DIM), jnp.bfloat16)], axis=1)
    for g in range(GROUP):
        at = head_columns(j * GROUP + g)
        scores = lax.dot_general(
            q_ref[:, at], key_tile, (((1,), (1,)), ((), ())), preferred_element_type=jnp.float32
        )
        scores = scores + bias
        top = jnp.broadcast_to(jnp.max(scores, axis=1, keepdims=True), (rows, HEAD_DIM))
        if state is not None:
            top_before = state[1][:, at]
            top = jnp.maximum(top, top_before)
        weights = jnp.concatenate(
            [jnp.exp2((scores[:, i : i + HEAD_DIM] - top) * EXP2_SCALE) for i in range(0, keys, HEAD_DIM)], axis=1
        )
        both = jnp.dot(weights.astype(jnp.bfloat16), value_tile, preferred_element_type=jnp.float32)
        acc, total = both[:, :HEAD_DIM], both[:, HEAD_DIM:]
        if state is not None:
            fade = jnp.exp2((top_before - top) * EXP2_SCALE)
            acc = acc + state[0][:, at] * fade
            total = total + state[2][:, at] * fade
        emit(at, acc, top, total)


def position_in(block, rows):
    return block * rows + lax.broadcasted_iota(jnp.int32, (rows, rows), 1)


def pack_kernel(k_hbm, v_hbm, kv_ref, sems):
    half = k_hbm.shape[1]
    copies = [
        pltpu.make_async_copy(src, kv_ref.at[:, pl.ds(i * half, half)], sems.at[i])
        for i, src in enumerate((k_hbm, v_hbm))
    ]
    for copy in copies:
        copy.start()
    for copy in copies:
        copy.wait()


def pack(keys, values):
    rows, half = keys.shape
    return pl.pallas_call(
        pack_kernel,
        out_shape=jax.ShapeDtypeStruct((rows, 2 * half), keys.dtype),
        in_specs=[HBM] * 2,
        out_specs=VMEM,
        scratch_shapes=[pltpu.SemaphoreType.DMA((2,))],
        compiler_params=pltpu.CompilerParams(vmem_limit_bytes=1024 * 1024),
    )(*(pltpu.with_memory_space_constraint(x, pltpu.HBM) for x in (keys, values)))


def first_kernel(doc_hbm, q_hbm, own, sib, back, back_sib, acc, top, total, q_ref, start_ref, doc_ref, doc_sem, q_sems):
    rows = q_ref.shape[0]
    small = pltpu.make_async_copy(doc_hbm, doc_ref, doc_sem)
    width = GROUP * HEAD_DIM
    large = [
        pltpu.make_async_copy(
            q_hbm.at[:, pl.ds(j * width, width)], q_ref.at[:, pl.ds(j * width, width)], q_sems.at[j]
        )
        for j in range(KV_HEADS)
    ]
    for copy in [small] + large:
        copy.start()
    plane, y, core = place()
    chip = 2 * plane + y
    position = (2 * chip + core) * rows + lax.broadcasted_iota(jnp.int32, (rows, rows), 0)
    small.wait()
    start = document_starts(doc_ref, position)
    start_ref[...] = start
    blocks = [2 * c + other for c in (chip, chip - 2) for other in (core, 1 - core)]
    keys = jnp.concatenate([position_in(block, rows) for block in blocks], axis=1)
    start, position = (jnp.concatenate([x] * len(blocks), axis=1) for x in (start, position))
    bias = jnp.where((keys >= start) & (keys <= position), 0.0, NEG)

    def emit(at, *new):
        acc[:, at], top[:, at], total[:, at] = new

    for j in range(KV_HEADS):
        large[j].wait()
        key_tile, value_tile = (
            jnp.concatenate([x[:, head_columns(head)] for x in (own, sib, back, back_sib)], axis=0)
            for head in (j, KV_HEADS + j)
        )
        update_heads(j, q_ref, key_tile, value_tile, bias, None, emit)


def attend_first(doc_lengths, queries, *blocks):
    rows = queries.shape[0]
    wide = jax.ShapeDtypeStruct(queries.shape, jnp.float32)
    return pl.pallas_call(
        first_kernel,
        out_shape=(wide, wide, wide, queries, jax.ShapeDtypeStruct((rows, rows), jnp.int32)),
        in_specs=[HBM] * 2 + [VMEM] * len(blocks),
        out_specs=(VMEM,) * 5,
        scratch_shapes=[
            pltpu.SMEM(doc_lengths.shape, jnp.int32),
            pltpu.SemaphoreType.DMA,
            pltpu.SemaphoreType.DMA((KV_HEADS,)),
        ],
        compiler_params=pltpu.CompilerParams(vmem_limit_bytes=20 * 1024 * 1024),
        cost_estimate=cost(rows, len(blocks)),
    )(*(pltpu.with_memory_space_constraint(x, pltpu.HBM) for x in (doc_lengths, queries)), *blocks)


def next_kernel(last, offsets, start_ref, q_ref, *refs):
    n_blocks = 2 * len(offsets)
    kv_refs, state, rest = refs[:n_blocks], refs[n_blocks : n_blocks + 3], refs[n_blocks + 3 :]
    rows = q_ref.shape[0]
    plane, y, core = place()
    chip = 2 * plane + y
    position = (2 * chip + core) * rows + lax.broadcasted_iota(jnp.int32, (rows, rows), 0)
    start = start_ref[...]
    blocks = [2 * (chip - offset) + other for offset in offsets for other in (core, 1 - core)]
    keys = [position_in(block, rows) for block in blocks]
    bias = jnp.concatenate([jnp.where((key >= start) & (key <= position), 0.0, NEG) for key in keys], axis=1)

    def tile(head):
        return jnp.concatenate([x[:, head_columns(head)] for x in kv_refs], axis=0)

    if last:
        out_hbm, out_ref, sems = rest

        def emit(at, acc, top, total):
            out_ref[:, at] = (acc / total).astype(jnp.bfloat16)
    else:

        def emit(at, *new):
            rest[0][:, at], rest[1][:, at], rest[2][:, at] = new

    copies = []
    for j in range(KV_HEADS):
        update_heads(j, q_ref, tile(j), tile(KV_HEADS + j), bias, state, emit)
        if last:
            at = head_columns(j * GROUP, GROUP)
            copies.append(pltpu.make_async_copy(out_ref.at[:, at], out_hbm.at[:, at], sems.at[j]))
            copies[-1].start()
    for copy in copies:
        copy.wait()


def attend_next(start, queries, blocks, offsets, state, last=False):
    rows = queries.shape[0]
    wide = jax.ShapeDtypeStruct(queries.shape, jnp.float32)
    scratch = []
    if last:
        scratch = [pltpu.VMEM(queries.shape, queries.dtype), pltpu.SemaphoreType.DMA((KV_HEADS,))]
    return pl.pallas_call(
        functools.partial(next_kernel, last, offsets),
        out_shape=jax.ShapeDtypeStruct(queries.shape, queries.dtype) if last else (wide,) * 3,
        in_specs=[VMEM] * (2 + len(blocks) + 3),
        out_specs=HBM if last else (VMEM,) * 3,
        scratch_shapes=scratch,
        compiler_params=pltpu.CompilerParams(vmem_limit_bytes=20 * 1024 * 1024),
        cost_estimate=cost(rows, len(blocks)),
    )(start, queries, *blocks, *state)


def cost(rows, blocks):
    keys = rows * blocks
    return pl.CostEstimate(
        flops=4 * rows * HEADS * HEAD_DIM * keys * 10,
        bytes_accessed=rows * HEADS * HEAD_DIM * 8,
        transcendentals=rows * HEADS * keys,
    )


def local(n, queries, keys, values, doc_lengths):
    reach = n // 2 // 4

    def permute(block, target):
        return lax.ppermute(block, "ctx", [(i, target(i)) for i in range(n)])

    def swap(block, bit):
        return permute(block, lambda i: i ^ bit)

    def onward(block, hop):
        fixed = 4 * (hop - 1)
        return permute(block, lambda i: i if i < fixed else fixed + (i - fixed + 4) % (n - fixed))

    def after(block, state):
        return lax.optimization_barrier((block, state))[0]

    def pair(block):
        return block, swap(block, 1)

    even = lax.axis_index("ctx") // 2 % 2 == 0
    own = pack(keys, values)
    column = [own, onward(own, 1)]
    if reach > 1:
        column.append(onward(column[1], 2))
    across = [swap(jnp.where(even, own, column[1]), 2)]
    *state, q, start = attend_first(doc_lengths, queries, *pair(own), *pair(column[1]))
    for z in range(2, reach + 1):
        if z < reach:
            column.append(onward(after(column[z], state[0]), z + 1))
        across.append(swap(after(jnp.where(even, after(column[z - 1], across[-1]), column[z]), state[0]), 2))
        blocks = pair(column[z]) + pair(after(across[z - 2], state[0]))
        state = attend_next(start, q, blocks, (2 * z, 2 * z - 3), state)
    return attend_next(start, q, pair(after(across[-1], state[0])), (2 * reach - 1,), state, last=True)


def solution(mesh):
    spec = P(("groups", "ctx"), None)
    return jax.shard_map(
        functools.partial(local, mesh.shape["ctx"]),
        mesh=mesh,
        in_specs=(spec, spec, spec, P("groups")),
        out_specs=spec,
        check_vma=False,
    )
```

time: 51.6 us -> 35.4 us (0.69)
  the two profiles are of different devices: /device:TPU:1 before, /device:TPU:9 now
where the time goes in v2:
time: 35.4 us; the launch traced here: 35.3 us
  waiting for transfers between devices  12.5 us (35%)
  Pallas kernels  11.6 us (33%)
  starting transfers between devices  11.1 us (31%)
    ppermute x9, waiting for transfers between devices, permute(): return lax.ppermute(block, 'ctx', [(i, target(i)) for i in range(n)])  12.5 us
    ppermute x9, starting transfers between devices, permute(): return lax.ppermute(block, 'ctx', [(i, target(i)) for i in range(n)])  11.1 us
    pallas_call x2, Pallas kernels, attend_next(): pl.pallas_call(functools.partial(next_kernel, last, offsets), out_shape=j...  5.74 us
    pallas_call x1, Pallas kernels, attend_first(): pl.pallas_call(first_kernel, out_shape=(wide, wide, wide, queries, jax.Sh...  4.83 us
    pallas_call x1, Pallas kernels, pack(): pl.pallas_call(pack_kernel, out_shape=jax.ShapeDtypeStruct((rows, 2 * hal...  0.98 us
  transfers between devices with their start and end apart: 9, of which 6 were waited for; matrix products, arithmetic and copies ran while one was open for 0% of the time, Pallas kernels for 22%

profile of v2, /device:TPU:9, one launch (start us, length us, event | category | flops | bytes accessed | tf_op | source)
XLA Modules:
  0.0 35.3 jit_solution(15015733314861635609)
XLA Ops:
  0.0 1.0 %shard_map.46.own = bf16[128,1024]{1,0:T(8,128)(2,1)S(1)} custom-call(bf16[128,512]{1,0:T(8,128)(2,1)} %k_hbm.1, bf16[128,512]{1,0:T(8,128)(2,1)} %v_hbm.1), custom_call_target="tpu_custom_call" | custom-call | tf_op jit(solution)/shard_map/pallas_call | solution.py:82
  1.0 1.3 %collective-permute-start.1 = (bf16[128,1024]{1,0:T(8,128)(2,1)S(1)}, bf16[128,1024]{1,0:T(8,128)(2,1)S(1)}, u32[]{:S(2)}, u32[]{:S(2)}) collective-permute-start(bf16[128,1024]{1,0:T(8,128)(2,1)S(1)} %shard_map.46.own), channel_id=1, source_target_pairs={{0,4},{1,5},{2,6},{3,7},{4,8},{5,9},{6,10},{7,11},{8,12},{9,13},{1... | collective-permute-start | bytes 786440 | tf_op jit(solution)/shard_map/ppermute | solution.py:211
  2.3 1.0 %collective-permute-start = (bf16[128,1024]{1,0:T(8,128)(2,1)S(1)}, bf16[128,1024]{1,0:T(8,128)(2,1)S(1)}, u32[]{:S(2)}, u32[]{:S(2)}) collective-permute-start(bf16[128,1024]{1,0:T(8,128)(2,1)S(1)} %shard_map.46.own), channel_id=1, source_target_pairs={{0,1},{1,0},{2,3},{3,2},{4,5},{5,4},{6,7},{7,6},{8,9},{9,8},{10,11... | collective-permute-start | bytes 786440 | tf_op jit(solution)/shard_map/ppermute | solution.py:211
  3.3 4.9 %collective-permute-done.1.back = bf16[128,1024]{1,0:T(8,128)(2,1)S(1)} collective-permute-done((bf16[128,1024]{1,0:T(8,128)(2,1)S(1)}, bf16[128,1024]{1,0:T(8,128)(2,1)S(1)}, u32[]{:S(2)}, u32[]{:S(2)}) %collective-permute-start.1) | collective-permute-done | bytes 262176 | tf_op jit(solution)/shard_map/ppermute | solution.py:211
  8.2 1.5 %collective-permute-start.2 = (bf16[128,1024]{1,0:T(8,128)(2,1)S(1)}, bf16[128,1024]{1,0:T(8,128)(2,1)S(1)}, u32[]{:S(2)}, u32[]{:S(2)}) collective-permute-start(bf16[128,1024]{1,0:T(8,128)(2,1)S(1)} %collective-permute-done.1.back), channel_id=1, source_target_pairs={{0,1},{1,0},{2,3},{3,2},{4,5},{5,4},{6,7},{7,6},{8,9},{9,8},{10,11... | collective-permute-start | bytes 786440 | tf_op jit(solution)/shard_map/ppermute | solution.py:211
  9.8 1.3 %collective-permute-start.3 = (bf16[128,1024]{1,0:T(8,128)(2,1)S(1)}, bf16[128,1024]{1,0:T(8,128)(2,1)S(1)}, u32[]{:S(2)}, u32[]{:S(2)}) collective-permute-start(bf16[128,1024]{1,0:T(8,128)(2,1)S(1)} %broadcast_select_fusion.1), channel_id=1, source_target_pairs={{0,2},{1,3},{2,0},{3,1},{4,6},{5,7},{6,4},{7,5},{8,10},{9,11},{10,... | collective-permute-start | bytes 786440 | tf_op jit(solution)/shard_map/ppermute | solution.py:211
  11.1 3.2 %collective-permute-start.4 = (bf16[128,1024]{1,0:T(8,128)(2,1)S(1)}, bf16[128,1024]{1,0:T(8,128)(2,1)S(1)}, u32[]{:S(2)}, u32[]{:S(2)}) collective-permute-start(bf16[128,1024]{1,0:T(8,128)(2,1)S(1)} %collective-permute-done.1.back), channel_id=1, source_target_pairs={{0,0},{1,1},{2,2},{3,3},{4,8},{5,9},{6,10},{7,11},{8,12},{9,13},{1... | collective-permute-start | bytes 786440 | tf_op jit(solution)/shard_map/ppermute | solution.py:211
  14.3 0.0 collective-permute-done.sib
  14.3 0.0 collective-permute-done.2.back_sib
  14.3 4.8 %shard_map.47 = (f32[128,4096]{1,0:T(8,128)S(1)}, f32[128,4096]{1,0:T(8,128)S(1)}, f32[128,4096]{1,0:T(8,128)S(1)}, bf16[128,4096]{1,0:T(8,128)(2,1)S(1)}, s32[128,128]{1,0:T(8,128)S(1)}) custom-call(s32[16]{0:T(128)} %doc_hbm.1, bf16[128,4096]{1,0:T(8,128)(2,1)} %q_hbm.1, bf16[128,1024]{1,0:T(8,128)(2,1)S(1)} %shard_map.46.own, ...), custom_call_target="tpu_custom_call" | custom-call | flops 10737418240 | bytes 4194304 | tf_op jit(solution)/shard_map/pallas_call | solution.py:130
  19.2 0.0 collective-permute-done.3.refs_2_
  19.2 2.3 %collective-permute-done.4.refs_0_ = bf16[128,1024]{1,0:T(8,128)(2,1)S(1)} collective-permute-done((bf16[128,1024]{1,0:T(8,128)(2,1)S(1)}, bf16[128,1024]{1,0:T(8,128)(2,1)S(1)}, u32[]{:S(2)}, u32[]{:S(2)}) %collective-permute-start.4) | collective-permute-done | bytes 262176 | tf_op jit(solution)/shard_map/ppermute | solution.py:211
  21.5 1.1 %collective-permute-start.6 = (bf16[128,1024]{1,0:T(8,128)(2,1)S(1)}, bf16[128,1024]{1,0:T(8,128)(2,1)S(1)}, u32[]{:S(2)}, u32[]{:S(2)}) collective-permute-start(bf16[128,1024]{1,0:T(8,128)(2,1)S(1)} %collective-permute-done.4.refs_0_), channel_id=1, source_target_pairs={{0,1},{1,0},{2,3},{3,2},{4,5},{5,4},{6,7},{7,6},{8,9},{9,8},{10,11... | collective-permute-start | bytes 786440 | tf_op jit(solution)/shard_map/ppermute | solution.py:211
  22.6 0.0 collective-permute-start.7
  22.6 0.3 collective-permute-start.5
  22.9 0.8 %collective-permute-done.6.refs_1_ = bf16[128,1024]{1,0:T(8,128)(2,1)S(1)} collective-permute-done((bf16[128,1024]{1,0:T(8,128)(2,1)S(1)}, bf16[128,1024]{1,0:T(8,128)(2,1)S(1)}, u32[]{:S(2)}, u32[]{:S(2)}) %collective-permute-start.6) | collective-permute-done | bytes 262176 | tf_op jit(solution)/shard_map/ppermute | solution.py:211
  23.8 0.4 %collective-permute-done.7.refs_3_ = bf16[128,1024]{1,0:T(8,128)(2,1)S(1)} collective-permute-done((bf16[128,1024]{1,0:T(8,128)(2,1)S(1)}, bf16[128,1024]{1,0:T(8,128)(2,1)S(1)}, u32[]{:S(2)}, u32[]{:S(2)}) %collective-permute-start.7) | collective-permute-done | bytes 262176 | tf_op jit(solution)/shard_map/ppermute | solution.py:211
  24.1 3.0 %shard_map.48 = (f32[128,4096]{1,0:T(8,128)S(1)}, f32[128,4096]{1,0:T(8,128)S(1)}, f32[128,4096]{1,0:T(8,128)S(1)}) custom-call(s32[128,128]{1,0:T(8,128)S(1)} %get-tuple-element.17.start_ref, bf16[128,4096]{1,0:T(8,128)(2,1)S(1)} %get-tuple-element.18.q_ref, bf16[128,1024]{1,0:T(8,128)(2,1)S(1)} %collective-permute-done.4.refs_0_, ...), custom_call_target="tpu_custom_call" | custom-call | flops 10737418240 | bytes 4194304 | tf_op jit(solution)/shard_map/pallas_call | solution.py:187
  27.2 2.9 %collective-permute-done.5.refs_0_ = bf16[128,1024]{1,0:T(8,128)(2,1)S(1)} collective-permute-done((bf16[128,1024]{1,0:T(8,128)(2,1)S(1)}, bf16[128,1024]{1,0:T(8,128)(2,1)S(1)}, u32[]{:S(2)}, u32[]{:S(2)}) %collective-permute-start.5) | collective-permute-done | bytes 262176 | tf_op jit(solution)/shard_map/ppermute | solution.py:211
  30.1 1.4 %collective-permute-start.8 = (bf16[128,1024]{1,0:T(8,128)(2,1)S(1)}, bf16[128,1024]{1,0:T(8,128)(2,1)S(1)}, u32[]{:S(2)}, u32[]{:S(2)}) collective-permute-start(bf16[128,1024]{1,0:T(8,128)(2,1)S(1)} %collective-permute-done.5.refs_0_), channel_id=1, source_target_pairs={{0,1},{1,0},{2,3},{3,2},{4,5},{5,4},{6,7},{7,6},{8,9},{9,8},{10,11... | collective-permute-start | bytes 786440 | tf_op jit(solution)/shard_map/ppermute | solution.py:211
  31.4 1.2 %collective-permute-done.8.refs_1_ = bf16[128,1024]{1,0:T(8,128)(2,1)S(1)} collective-permute-done((bf16[128,1024]{1,0:T(8,128)(2,1)S(1)}, bf16[128,1024]{1,0:T(8,128)(2,1)S(1)}, u32[]{:S(2)}, u32[]{:S(2)}) %collective-permute-start.8) | collective-permute-done | bytes 262176 | tf_op jit(solution)/shard_map/ppermute | solution.py:211
  32.6 2.7 %shard_map.49 = bf16[128,4096]{1,0:T(8,128)(2,1)} custom-call(s32[128,128]{1,0:T(8,128)S(1)} %get-tuple-element.17.start_ref, bf16[128,4096]{1,0:T(8,128)(2,1)S(1)} %get-tuple-element.18.q_ref, bf16[128,1024]{1,0:T(8,128)(2,1)S(1)} %collective-permute-done.5.refs_0_, bf16[128,1024]{1,0:T(8,128)(2,1)S(1)} %collective-permute-done.8.refs_1_, ...), custom_call_target="tpu_custom_call" | custom-call | flops 5368709120 | bytes 4194304 | tf_op jit(solution)/shard_map/pallas_call | solution.py:187
  (2 shorter events, 0.1 us)
Async XLA Ops:
  1.0 7.2 %collective-permute-start.1 = (bf16[128,1024]{1,0:T(8,128)(2,1)S(1)}, bf16[128,1024]{1,0:T(8,128)(2,1)S(1)}, u32[]{:S(2)}, u32[]{:S(2)}) collective-permute-start(bf16[128,1024]{1,0:T(8,128)(2,1)S(1)} %shard_map.46.own), channel_id=1, source_target_pairs={{0,4},{1,5},{2,6},{3,7},{4,8},{5,9},{6,10},{7,11},{8,12},{9,13},{1... | collective-permute-start | bytes 786440 | tf_op jit(solution)/shard_map/ppermute | solution.py:211
  2.3 12.0 %collective-permute-start = (bf16[128,1024]{1,0:T(8,128)(2,1)S(1)}, bf16[128,1024]{1,0:T(8,128)(2,1)S(1)}, u32[]{:S(2)}, u32[]{:S(2)}) collective-permute-start(bf16[128,1024]{1,0:T(8,128)(2,1)S(1)} %shard_map.46.own), channel_id=1, source_target_pairs={{0,1},{1,0},{2,3},{3,2},{4,5},{5,4},{6,7},{7,6},{8,9},{9,8},{10,11... | collective-permute-start | bytes 786440 | tf_op jit(solution)/shard_map/ppermute | solution.py:211
  8.2 6.1 %collective-permute-start.2 = (bf16[128,1024]{1,0:T(8,128)(2,1)S(1)}, bf16[128,1024]{1,0:T(8,128)(2,1)S(1)}, u32[]{:S(2)}, u32[]{:S(2)}) collective-permute-start(bf16[128,1024]{1,0:T(8,128)(2,1)S(1)} %collective-permute-done.1.back), channel_id=1, source_target_pairs={{0,1},{1,0},{2,3},{3,2},{4,5},{5,4},{6,7},{7,6},{8,9},{9,8},{10,11... | collective-permute-start | bytes 786440 | tf_op jit(solution)/shard_map/ppermute | solution.py:211
  9.8 9.4 %collective-permute-start.3 = (bf16[128,1024]{1,0:T(8,128)(2,1)S(1)}, bf16[128,1024]{1,0:T(8,128)(2,1)S(1)}, u32[]{:S(2)}, u32[]{:S(2)}) collective-permute-start(bf16[128,1024]{1,0:T(8,128)(2,1)S(1)} %broadcast_select_fusion.1), channel_id=1, source_target_pairs={{0,2},{1,3},{2,0},{3,1},{4,6},{5,7},{6,4},{7,5},{8,10},{9,11},{10,... | collective-permute-start | bytes 786440 | tf_op jit(solution)/shard_map/ppermute | solution.py:211
  11.1 10.4 %collective-permute-start.4 = (bf16[128,1024]{1,0:T(8,128)(2,1)S(1)}, bf16[128,1024]{1,0:T(8,128)(2,1)S(1)}, u32[]{:S(2)}, u32[]{:S(2)}) collective-permute-start(bf16[128,1024]{1,0:T(8,128)(2,1)S(1)} %collective-permute-done.1.back), channel_id=1, source_target_pairs={{0,0},{1,1},{2,2},{3,3},{4,8},{5,9},{6,10},{7,11},{8,12},{9,13},{1... | collective-permute-start | bytes 786440 | tf_op jit(solution)/shard_map/ppermute | solution.py:211
  21.5 2.3 %collective-permute-start.6 = (bf16[128,1024]{1,0:T(8,128)(2,1)S(1)}, bf16[128,1024]{1,0:T(8,128)(2,1)S(1)}, u32[]{:S(2)}, u32[]{:S(2)}) collective-permute-start(bf16[128,1024]{1,0:T(8,128)(2,1)S(1)} %collective-permute-done.4.refs_0_), channel_id=1, source_target_pairs={{0,1},{1,0},{2,3},{3,2},{4,5},{5,4},{6,7},{7,6},{8,9},{9,8},{10,11... | collective-permute-start | bytes 786440 | tf_op jit(solution)/shard_map/ppermute | solution.py:211
  22.6 1.5 %collective-permute-start.7 = (bf16[128,1024]{1,0:T(8,128)(2,1)S(1)}, bf16[128,1024]{1,0:T(8,128)(2,1)S(1)}, u32[]{:S(2)}, u32[]{:S(2)}) collective-permute-start(bf16[128,1024]{1,0:T(8,128)(2,1)S(1)} %collective-permute-done.3.refs_2_), channel_id=1, source_target_pairs={{0,1},{1,0},{2,3},{3,2},{4,5},{5,4},{6,7},{7,6},{8,9},{9,8},{10,11... | collective-permute-start | bytes 786440 | tf_op jit(solution)/shard_map/ppermute | solution.py:211
  22.6 7.4 %collective-permute-start.5 = (bf16[128,1024]{1,0:T(8,128)(2,1)S(1)}, bf16[128,1024]{1,0:T(8,128)(2,1)S(1)}, u32[]{:S(2)}, u32[]{:S(2)}) collective-permute-start(bf16[128,1024]{1,0:T(8,128)(2,1)S(1)} %broadcast_select_fusion), channel_id=1, source_target_pairs={{0,2},{1,3},{2,0},{3,1},{4,6},{5,7},{6,4},{7,5},{8,10},{9,11},{10,... | collective-permute-start | bytes 786440 | tf_op jit(solution)/shard_map/ppermute | solution.py:211
  30.1 2.5 %collective-permute-start.8 = (bf16[128,1024]{1,0:T(8,128)(2,1)S(1)}, bf16[128,1024]{1,0:T(8,128)(2,1)S(1)}, u32[]{:S(2)}, u32[]{:S(2)}) collective-permute-start(bf16[128,1024]{1,0:T(8,128)(2,1)S(1)} %collective-permute-done.5.refs_0_), channel_id=1, source_target_pairs={{0,1},{1,0},{2,3},{3,2},{4,5},{5,4},{6,7},{7,6},{8,9},{9,8},{10,11... | collective-permute-start | bytes 786440 | tf_op jit(solution)/shard_map/ppermute | solution.py:211

commit v3 on v2

--- a/solution.py
+++ b/solution.py
@@ -213,30 +213,33 @@
     def swap(block, bit):
         return permute(block, lambda i: i ^ bit)
 
-    def onward(block, hop):
+    def onward(block, step, hop):
         fixed = 4 * (hop - 1)
-        return permute(block, lambda i: i if i < fixed else fixed + (i - fixed + 4) % (n - fixed))
-
-    def after(block, state):
-        return lax.optimization_barrier((block, state))[0]
+        return permute(block, lambda i: i ^ 1 if i < fixed else fixed + (i - fixed + step) % (n - fixed))
+
+    def after(block, other):
+        return lax.optimization_barrier((block, other))[0]
 
     def pair(block):
         return block, swap(block, 1)
 
     even = lax.axis_index("ctx") // 2 % 2 == 0
     own = pack(keys, values)
-    column = [own, onward(own, 1)]
-    if reach > 1:
-        column.append(onward(column[1], 2))
-    across = [swap(jnp.where(even, own, column[1]), 2)]
-    *state, q, start = attend_first(doc_lengths, queries, *pair(own), *pair(column[1]))
+    back = onward(own, 4, 1)
+    far = [(onward(back, 4, 2), onward(back, 2, 2))] if reach > 1 else []
+    back_pair = pair(back)
+    across = swap(jnp.where(even, own, after(back, back_pair[1])), 2)
+    *state, q, start = attend_first(doc_lengths, queries, *pair(own), *back_pair)
+    blocks, offsets = (across,), (1,)
     for z in range(2, reach + 1):
+        here, beside = (after(block, state[0]) for block in far[-1])
+        blocks, offsets = blocks + (here, beside), offsets + (2 * z, 2 * z - 1)
         if z < reach:
-            column.append(onward(after(column[z], state[0]), z + 1))
-        across.append(swap(after(jnp.where(even, after(column[z - 1], across[-1]), column[z]), state[0]), 2))
-        blocks = pair(column[z]) + pair(after(across[z - 2], state[0]))
-        state = attend_next(start, q, blocks, (2 * z, 2 * z - 3), state)
-    return attend_next(start, q, pair(after(across[-1], state[0])), (2 * reach - 1,), state, last=True)
+            far.append((onward(here, 4, z + 1), onward(here, 2, z + 1)))
+            state = attend_next(start, q, [x for block in blocks for x in pair(block)], offsets, state)
+            blocks, offsets = (), ()
+    blocks = [x for block in blocks for x in pair(after(block, state[0]))]
+    return attend_next(start, q, blocks, offsets, state, last=True)
 
 
 def solution(mesh):

time: 35.4 us -> 32.7 us (0.924)
  the two profiles are of different devices: /device:TPU:9 before, /device:TPU:11 now
where the time goes in v3:
time: 32.7 us; the launch traced here: 32.6 us
  waiting for transfers between devices  11.6 us (35%)
  Pallas kernels  11.3 us (35%)
  starting transfers between devices  9.58 us (29%)
    ppermute x9, waiting for transfers between devices, permute(): return lax.ppermute(block, 'ctx', [(i, target(i)) for i in range(n)])  11.6 us
    ppermute x9, starting transfers between devices, permute(): return lax.ppermute(block, 'ctx', [(i, target(i)) for i in range(n)])  9.58 us
    pallas_call x1, Pallas kernels, attend_next(): pl.pallas_call(functools.partial(next_kernel, last, offsets), out_shape=j...  5.49 us
    pallas_call x1, Pallas kernels, attend_first(): pl.pallas_call(first_kernel, out_shape=(wide, wide, wide, queries, jax.Sh...  4.83 us
    pallas_call x1, Pallas kernels, pack(): pl.pallas_call(pack_kernel, out_shape=jax.ShapeDtypeStruct((rows, 2 * hal...  0.98 us
  transfers between devices with their start and end apart: 9, of which 4 were waited for; matrix products, arithmetic and copies ran while one was open for 0% of the time, Pallas kernels for 15%

profile of v3, /device:TPU:11, one launch (start us, length us, event | category | flops | bytes accessed | tf_op | source)
XLA Modules:
  0.0 32.6 jit_solution(7077724889808346574)
XLA Ops:
  0.0 1.0 %shard_map.46.own = bf16[128,1024]{1,0:T(8,128)(2,1)S(1)} custom-call(bf16[128,512]{1,0:T(8,128)(2,1)} %k_hbm.1, bf16[128,512]{1,0:T(8,128)(2,1)} %v_hbm.1), custom_call_target="tpu_custom_call" | custom-call | tf_op jit(solution)/shard_map/pallas_call | solution.py:82
  1.0 1.3 %collective-permute-start.1 = (bf16[128,1024]{1,0:T(8,128)(2,1)S(1)}, bf16[128,1024]{1,0:T(8,128)(2,1)S(1)}, u32[]{:S(2)}, u32[]{:S(2)}) collective-permute-start(bf16[128,1024]{1,0:T(8,128)(2,1)S(1)} %shard_map.46.own), channel_id=1, source_target_pairs={{0,4},{1,5},{2,6},{3,7},{4,8},{5,9},{6,10},{7,11},{8,12},{9,13},{1... | collective-permute-start | bytes 786440 | tf_op jit(solution)/shard_map/ppermute | solution.py:211
  2.3 5.9 %collective-permute-done.1.back = bf16[128,1024]{1,0:T(8,128)(2,1)S(1)} collective-permute-done((bf16[128,1024]{1,0:T(8,128)(2,1)S(1)}, bf16[128,1024]{1,0:T(8,128)(2,1)S(1)}, u32[]{:S(2)}, u32[]{:S(2)}) %collective-permute-start.1) | collective-permute-done | bytes 262176 | tf_op jit(solution)/shard_map/ppermute | solution.py:211
  8.2 1.5 %collective-permute-start.2 = (bf16[128,1024]{1,0:T(8,128)(2,1)S(1)}, bf16[128,1024]{1,0:T(8,128)(2,1)S(1)}, u32[]{:S(2)}, u32[]{:S(2)}) collective-permute-start(bf16[128,1024]{1,0:T(8,128)(2,1)S(1)} %collective-permute-done.1.back), channel_id=1, source_target_pairs={{0,1},{1,0},{2,3},{3,2},{4,5},{5,4},{6,7},{7,6},{8,9},{9,8},{10,11... | collective-permute-start | bytes 786440 | tf_op jit(solution)/shard_map/ppermute | solution.py:211
  9.8 0.0 collective-permute-start
  9.8 1.2 %collective-permute-start.7 = (bf16[128,1024]{1,0:T(8,128)(2,1)S(1)}, bf16[128,1024]{1,0:T(8,128)(2,1)S(1)}, u32[]{:S(2)}, u32[]{:S(2)}) collective-permute-start(bf16[128,1024]{1,0:T(8,128)(2,1)S(1)} %collective-permute-done.1.back), channel_id=1, source_target_pairs={{0,1},{1,0},{2,3},{3,2},{4,6},{5,7},{6,8},{7,9},{8,10},{9,11},{10,... | collective-permute-start | bytes 786440 | tf_op jit(solution)/shard_map/ppermute | solution.py:211
  11.0 1.3 %collective-permute-start.5 = (bf16[128,1024]{1,0:T(8,128)(2,1)S(1)}, bf16[128,1024]{1,0:T(8,128)(2,1)S(1)}, u32[]{:S(2)}, u32[]{:S(2)}) collective-permute-start(bf16[128,1024]{1,0:T(8,128)(2,1)S(1)} %collective-permute-done.1.back), channel_id=1, source_target_pairs={{0,1},{1,0},{2,3},{3,2},{4,8},{5,9},{6,10},{7,11},{8,12},{9,13},{1... | collective-permute-start | bytes 786440 | tf_op jit(solution)/shard_map/ppermute | solution.py:211
  12.3 0.0 collective-permute-done.2.back_sib
  12.3 1.3 %collective-permute-start.3 = (bf16[128,1024]{1,0:T(8,128)(2,1)S(1)}, bf16[128,1024]{1,0:T(8,128)(2,1)S(1)}, u32[]{:S(2)}, u32[]{:S(2)}) collective-permute-start(bf16[128,1024]{1,0:T(8,128)(2,1)S(1)} %broadcast_select_fusion), channel_id=1, source_target_pairs={{0,2},{1,3},{2,0},{3,1},{4,6},{5,7},{6,4},{7,5},{8,10},{9,11},{10,... | collective-permute-start | bytes 786440 | tf_op jit(solution)/shard_map/ppermute | solution.py:211
  13.6 0.0 collective-permute-done.sib
  13.7 4.8 %shard_map.47 = (f32[128,4096]{1,0:T(8,128)S(1)}, f32[128,4096]{1,0:T(8,128)S(1)}, f32[128,4096]{1,0:T(8,128)S(1)}, bf16[128,4096]{1,0:T(8,128)(2,1)S(1)}, s32[128,128]{1,0:T(8,128)S(1)}) custom-call(s32[16]{0:T(128)} %doc_hbm.1, bf16[128,4096]{1,0:T(8,128)(2,1)} %q_hbm.1, bf16[128,1024]{1,0:T(8,128)(2,1)S(1)} %shard_map.46.own, ...), custom_call_target="tpu_custom_call" | custom-call | flops 10737418240 | bytes 4194304 | tf_op jit(solution)/shard_map/pallas_call | solution.py:130
  18.5 0.4 %collective-permute-done.7.refs_4_ = bf16[128,1024]{1,0:T(8,128)(2,1)S(1)} collective-permute-done((bf16[128,1024]{1,0:T(8,128)(2,1)S(1)}, bf16[128,1024]{1,0:T(8,128)(2,1)S(1)}, u32[]{:S(2)}, u32[]{:S(2)}) %collective-permute-start.7) | collective-permute-done | bytes 262176 | tf_op jit(solution)/shard_map/ppermute | solution.py:211
  18.9 0.0 collective-permute-done.5.refs_2_
  19.0 2.3 %collective-permute-start.6 = (bf16[128,1024]{1,0:T(8,128)(2,1)S(1)}, bf16[128,1024]{1,0:T(8,128)(2,1)S(1)}, u32[]{:S(2)}, u32[]{:S(2)}) collective-permute-start(bf16[128,1024]{1,0:T(8,128)(2,1)S(1)} %collective-permute-done.5.refs_2_), channel_id=1, source_target_pairs={{0,1},{1,0},{2,3},{3,2},{4,5},{5,4},{6,7},{7,6},{8,9},{9,8},{10,11... | collective-permute-start | bytes 786440 | tf_op jit(solution)/shard_map/ppermute | solution.py:211
  21.3 0.0 collective-permute-start.8
  21.3 4.1 %collective-permute-done.3.refs_0_ = bf16[128,1024]{1,0:T(8,128)(2,1)S(1)} collective-permute-done((bf16[128,1024]{1,0:T(8,128)(2,1)S(1)}, bf16[128,1024]{1,0:T(8,128)(2,1)S(1)}, u32[]{:S(2)}, u32[]{:S(2)}) %collective-permute-start.3) | collective-permute-done | bytes 262176 | tf_op jit(solution)/shard_map/ppermute | solution.py:211
  25.4 0.5 %collective-permute-start.4 = (bf16[128,1024]{1,0:T(8,128)(2,1)S(1)}, bf16[128,1024]{1,0:T(8,128)(2,1)S(1)}, u32[]{:S(2)}, u32[]{:S(2)}) collective-permute-start(bf16[128,1024]{1,0:T(8,128)(2,1)S(1)} %collective-permute-done.3.refs_0_), channel_id=1, source_target_pairs={{0,1},{1,0},{2,3},{3,2},{4,5},{5,4},{6,7},{7,6},{8,9},{9,8},{10,11... | collective-permute-start | bytes 786440 | tf_op jit(solution)/shard_map/ppermute | solution.py:211
  25.9 0.0 collective-permute-done.6.refs_3_
  25.9 0.0 collective-permute-done.8.refs_5_
  25.9 1.2 %collective-permute-done.4.refs_1_ = bf16[128,1024]{1,0:T(8,128)(2,1)S(1)} collective-permute-done((bf16[128,1024]{1,0:T(8,128)(2,1)S(1)}, bf16[128,1024]{1,0:T(8,128)(2,1)S(1)}, u32[]{:S(2)}, u32[]{:S(2)}) %collective-permute-start.4) | collective-permute-done | bytes 262176 | tf_op jit(solution)/shard_map/ppermute | solution.py:211
  27.1 5.5 %shard_map.48 = bf16[128,4096]{1,0:T(8,128)(2,1)} custom-call(s32[128,128]{1,0:T(8,128)S(1)} %get-tuple-element.16.start_ref, bf16[128,4096]{1,0:T(8,128)(2,1)S(1)} %get-tuple-element.17.q_ref, bf16[128,1024]{1,0:T(8,128)(2,1)S(1)} %collective-permute-done.3.refs_0_, bf16[128,1024]{1,0:T(8,128)(2,1)S(1)} %collective-permute-done.4.refs_1_, ...), custom_call_target="tpu_custom_call" | custom-call | flops 16106127360 | bytes 4194304 | tf_op jit(solution)/shard_map/pallas_call | solution.py:187
  (1 shorter events, 0.0 us)
Async XLA Ops:
  1.0 7.2 %collective-permute-start.1 = (bf16[128,1024]{1,0:T(8,128)(2,1)S(1)}, bf16[128,1024]{1,0:T(8,128)(2,1)S(1)}, u32[]{:S(2)}, u32[]{:S(2)}) collective-permute-start(bf16[128,1024]{1,0:T(8,128)(2,1)S(1)} %shard_map.46.own), channel_id=1, source_target_pairs={{0,4},{1,5},{2,6},{3,7},{4,8},{5,9},{6,10},{7,11},{8,12},{9,13},{1... | collective-permute-start | bytes 786440 | tf_op jit(solution)/shard_map/ppermute | solution.py:211
  8.2 4.1 %collective-permute-start.2 = (bf16[128,1024]{1,0:T(8,128)(2,1)S(1)}, bf16[128,1024]{1,0:T(8,128)(2,1)S(1)}, u32[]{:S(2)}, u32[]{:S(2)}) collective-permute-start(bf16[128,1024]{1,0:T(8,128)(2,1)S(1)} %collective-permute-done.1.back), channel_id=1, source_target_pairs={{0,1},{1,0},{2,3},{3,2},{4,5},{5,4},{6,7},{7,6},{8,9},{9,8},{10,11... | collective-permute-start | bytes 786440 | tf_op jit(solution)/shard_map/ppermute | solution.py:211
  9.8 3.9 %collective-permute-start = (bf16[128,1024]{1,0:T(8,128)(2,1)S(1)}, bf16[128,1024]{1,0:T(8,128)(2,1)S(1)}, u32[]{:S(2)}, u32[]{:S(2)}) collective-permute-start(bf16[128,1024]{1,0:T(8,128)(2,1)S(1)} %shard_map.46.own), channel_id=1, source_target_pairs={{0,1},{1,0},{2,3},{3,2},{4,5},{5,4},{6,7},{7,6},{8,9},{9,8},{10,11... | collective-permute-start | bytes 786440 | tf_op jit(solution)/shard_map/ppermute | solution.py:211
  9.8 9.2 %collective-permute-start.7 = (bf16[128,1024]{1,0:T(8,128)(2,1)S(1)}, bf16[128,1024]{1,0:T(8,128)(2,1)S(1)}, u32[]{:S(2)}, u32[]{:S(2)}) collective-permute-start(bf16[128,1024]{1,0:T(8,128)(2,1)S(1)} %collective-permute-done.1.back), channel_id=1, source_target_pairs={{0,1},{1,0},{2,3},{3,2},{4,6},{5,7},{6,8},{7,9},{8,10},{9,11},{10,... | collective-permute-start | bytes 786440 | tf_op jit(solution)/shard_map/ppermute | solution.py:211
  11.0 7.9 %collective-permute-start.5 = (bf16[128,1024]{1,0:T(8,128)(2,1)S(1)}, bf16[128,1024]{1,0:T(8,128)(2,1)S(1)}, u32[]{:S(2)}, u32[]{:S(2)}) collective-permute-start(bf16[128,1024]{1,0:T(8,128)(2,1)S(1)} %collective-permute-done.1.back), channel_id=1, source_target_pairs={{0,1},{1,0},{2,3},{3,2},{4,8},{5,9},{6,10},{7,11},{8,12},{9,13},{1... | collective-permute-start | bytes 786440 | tf_op jit(solution)/shard_map/ppermute | solution.py:211
  12.3 13.1 %collective-permute-start.3 = (bf16[128,1024]{1,0:T(8,128)(2,1)S(1)}, bf16[128,1024]{1,0:T(8,128)(2,1)S(1)}, u32[]{:S(2)}, u32[]{:S(2)}) collective-permute-start(bf16[128,1024]{1,0:T(8,128)(2,1)S(1)} %broadcast_select_fusion), channel_id=1, source_target_pairs={{0,2},{1,3},{2,0},{3,1},{4,6},{5,7},{6,4},{7,5},{8,10},{9,11},{10,... | collective-permute-start | bytes 786440 | tf_op jit(solution)/shard_map/ppermute | solution.py:211
  19.0 7.0 %collective-permute-start.6 = (bf16[128,1024]{1,0:T(8,128)(2,1)S(1)}, bf16[128,1024]{1,0:T(8,128)(2,1)S(1)}, u32[]{:S(2)}, u32[]{:S(2)}) collective-permute-start(bf16[128,1024]{1,0:T(8,128)(2,1)S(1)} %collective-permute-done.5.refs_2_), channel_id=1, source_target_pairs={{0,1},{1,0},{2,3},{3,2},{4,5},{5,4},{6,7},{7,6},{8,9},{9,8},{10,11... | collective-permute-start | bytes 786440 | tf_op jit(solution)/shard_map/ppermute | solution.py:211
  21.3 4.6 %collective-permute-start.8 = (bf16[128,1024]{1,0:T(8,128)(2,1)S(1)}, bf16[128,1024]{1,0:T(8,128)(2,1)S(1)}, u32[]{:S(2)}, u32[]{:S(2)}) collective-permute-start(bf16[128,1024]{1,0:T(8,128)(2,1)S(1)} %collective-permute-done.7.refs_4_), channel_id=1, source_target_pairs={{0,1},{1,0},{2,3},{3,2},{4,5},{5,4},{6,7},{7,6},{8,9},{9,8},{10,11... | collective-permute-start | bytes 786440 | tf_op jit(solution)/shard_map/ppermute | solution.py:211
  25.4 1.7 %collective-permute-start.4 = (bf16[128,1024]{1,0:T(8,128)(2,1)S(1)}, bf16[128,1024]{1,0:T(8,128)(2,1)S(1)}, u32[]{:S(2)}, u32[]{:S(2)}) collective-permute-start(bf16[128,1024]{1,0:T(8,128)(2,1)S(1)} %collective-permute-done.3.refs_0_), channel_id=1, source_target_pairs={{0,1},{1,0},{2,3},{3,2},{4,5},{5,4},{6,7},{7,6},{8,9},{9,8},{10,11... | collective-permute-start | bytes 786440 | tf_op jit(solution)/shard_map/ppermute | solution.py:211

commit v4 on v3

--- a/solution.py
+++ b/solution.py
@@ -142,20 +142,15 @@
     )(*(pltpu.with_memory_space_constraint(x, pltpu.HBM) for x in (doc_lengths, queries)), *blocks)
 
 
-def next_kernel(last, offsets, start_ref, q_ref, *refs):
-    n_blocks = 2 * len(offsets)
+def next_kernel(last, places, start_ref, q_ref, *refs):
+    n_blocks = len(places)
     kv_refs, state, rest = refs[:n_blocks], refs[n_blocks : n_blocks + 3], refs[n_blocks + 3 :]
     rows = q_ref.shape[0]
     plane, y, core = place()
     chip = 2 * plane + y
     position = (2 * chip + core) * rows + lax.broadcasted_iota(jnp.int32, (rows, rows), 0)
     start = start_ref[...]
-    blocks = [2 * (chip - offset) + other for offset in offsets for other in (core, 1 - core)]
-    keys = [position_in(block, rows) for block in blocks]
-    bias = jnp.concatenate([jnp.where((key >= start) & (key <= position), 0.0, NEG) for key in keys], axis=1)
-
-    def tile(head):
-        return jnp.concatenate([x[:, head_columns(head)] for x in kv_refs], axis=0)
+    first_start = jnp.min(start[:8])
 
     if last:
         out_hbm, out_ref, sems = rest
@@ -167,25 +162,58 @@
         def emit(at, *new):
             rest[0][:, at], rest[1][:, at], rest[2][:, at] = new
 
-    copies = []
-    for j in range(KV_HEADS):
-        update_heads(j, q_ref, tile(j), tile(KV_HEADS + j), bias, state, emit)
-        if last:
-            at = head_columns(j * GROUP, GROUP)
-            copies.append(pltpu.make_async_copy(out_ref.at[:, at], out_hbm.at[:, at], sems.at[j]))
-            copies[-1].start()
-    for copy in copies:
-        copy.wait()
-
-
-def attend_next(start, queries, blocks, offsets, state, last=False):
+    def out_copy(j):
+        at = head_columns(j * GROUP, GROUP)
+        return pltpu.make_async_copy(out_ref.at[:, at], out_hbm.at[:, at], sems.at[j])
+
+    def update(used):
+        if used:
+            keys = [position_in(2 * (chip - places[b][0]) + (core ^ places[b][1]), rows) for b in used]
+            bias = [jnp.where((key >= start) & (key <= position), 0.0, NEG) for key in keys]
+            bias = jnp.concatenate(bias, axis=1)
+        for j in range(KV_HEADS):
+            if used:
+                key_tile, value_tile = (
+                    jnp.concatenate([kv_refs[b][:, head_columns(head)] for b in used], axis=0)
+                    for head in (j, KV_HEADS + j)
+                )
+                update_heads(j, q_ref, key_tile, value_tile, bias, state, emit)
+            else:
+                for g in range(GROUP):
+                    at = head_columns(j * GROUP + g)
+                    emit(at, *(x[:, at] for x in state))
+            if last:
+                out_copy(j).start()
+
+    every = list(range(n_blocks))
+    near = [b for b in every if places[b][0] == min(places)[0]]
+    further = [offset for offset, _ in places if offset > min(places)[0]]
+
+    def seen(offset):
+        return (2 * (chip - offset) + 2) * rows > first_start
+
+    seen_near = seen(min(places)[0])
+    pl.when(jnp.logical_not(seen_near))(lambda: update([]))
+    if further and len(near) > 1:
+        seen_all = seen(min(further))
+        pl.when(seen_near & jnp.logical_not(seen_all))(lambda: update(near))
+        pl.when(seen_all)(lambda: update(every))
+    else:
+        pl.when(seen_near)(lambda: update(every))
+
+    if last:
+        for j in range(KV_HEADS):
+            out_copy(j).wait()
+
+
+def attend_next(start, queries, blocks, places, state, last=False):
     rows = queries.shape[0]
     wide = jax.ShapeDtypeStruct(queries.shape, jnp.float32)
     scratch = []
     if last:
         scratch = [pltpu.VMEM(queries.shape, queries.dtype), pltpu.SemaphoreType.DMA((KV_HEADS,))]
     return pl.pallas_call(
-        functools.partial(next_kernel, last, offsets),
+        functools.partial(next_kernel, last, places),
         out_shape=jax.ShapeDtypeStruct(queries.shape, queries.dtype) if last else (wide,) * 3,
         in_specs=[VMEM] * (2 + len(blocks) + 3),
         out_specs=HBM if last else (VMEM,) * 3,
@@ -223,23 +251,25 @@
     def pair(block):
         return block, swap(block, 1)
 
+    own = pack(keys, values)
+    beside = swap(own, 2)
+    back = onward(own, 4, 1)
+    back_beside = permute(beside, lambda i: i ^ 1 if i // 2 % 2 else (i + 4) % n)
+    far = (onward(back, 4, 2), onward(back, 2, 2)) if reach > 1 else ()
+    *state, q, start = attend_first(doc_lengths, queries, *pair(own), *pair(back))
+    back_beside, beside, far = after((back_beside, beside, far), state[0])
     even = lax.axis_index("ctx") // 2 % 2 == 0
-    own = pack(keys, values)
-    back = onward(own, 4, 1)
-    far = [(onward(back, 4, 2), onward(back, 2, 2))] if reach > 1 else []
-    back_pair = pair(back)
-    across = swap(jnp.where(even, own, after(back, back_pair[1])), 2)
-    *state, q, start = attend_first(doc_lengths, queries, *pair(own), *back_pair)
-    blocks, offsets = (across,), (1,)
+    blocks, places = pair(jnp.where(even, back_beside, beside)), ((1, 0), (1, 1))
     for z in range(2, reach + 1):
-        here, beside = (after(block, state[0]) for block in far[-1])
-        blocks, offsets = blocks + (here, beside), offsets + (2 * z, 2 * z - 1)
+        here, other = far, tuple(swap(block, 1) for block in far)
         if z < reach:
-            far.append((onward(here, 4, z + 1), onward(here, 2, z + 1)))
-            state = attend_next(start, q, [x for block in blocks for x in pair(block)], offsets, state)
-            blocks, offsets = (), ()
-    blocks = [x for block in blocks for x in pair(after(block, state[0]))]
-    return attend_next(start, q, blocks, offsets, state, last=True)
+            far = after((onward(far[0], 4, z + 1), onward(far[0], 2, z + 1)), state[0])
+        state = attend_next(start, q, here, ((2 * z, 0), (2 * z - 1, 0)), state)
+        blocks, places = blocks + other, places + ((2 * z, 1), (2 * z - 1, 1))
+        if z < reach:
+            state = attend_next(start, q, blocks, places, state)
+            blocks, places = (), ()
+    return attend_next(start, q, blocks, places, state, last=True)
 
 
 def solution(mesh):

time: 32.7 us -> 32.3 us (0.988)
  the two profiles are of different devices: /device:TPU:11 before, /device:TPU:27 now
where the time goes in v4:
time: 32.3 us; the launch traced here: 32.2 us
  Pallas kernels  12.1 us (37%)
  waiting for transfers between devices  12.1 us (37%)
  starting transfers between devices  7.68 us (24%)
    ppermute x10, waiting for transfers between devices, permute(): return lax.ppermute(block, 'ctx', [(i, target(i)) for i in range(n)])  12.1 us
    ppermute x10, starting transfers between devices, permute(): return lax.ppermute(block, 'ctx', [(i, target(i)) for i in range(n)])  7.68 us
    pallas_call x2, Pallas kernels, attend_next(): pl.pallas_call(functools.partial(next_kernel, last, places), out_shape=ja...  6.3 us
    pallas_call x1, Pallas kernels, attend_first(): pl.pallas_call(first_kernel, out_shape=(wide, wide, wide, queries, jax.Sh...  4.83 us
    pallas_call x1, Pallas kernels, pack(): pl.pallas_call(pack_kernel, out_shape=jax.ShapeDtypeStruct((rows, 2 * hal...  0.98 us
  transfers between devices with their start and end apart: 10, of which 3 were waited for; matrix products, arithmetic and copies ran while one was open for 0% of the time, Pallas kernels for 22%

profile of v4, /device:TPU:27, one launch (start us, length us, event | category | flops | bytes accessed | tf_op | source)
XLA Modules:
  0.0 32.2 jit_solution(8861526474928751868)
XLA Ops:
  0.0 1.0 %shard_map.46.own = bf16[128,1024]{1,0:T(8,128)(2,1)S(1)} custom-call(bf16[128,512]{1,0:T(8,128)(2,1)} %k_hbm.1, bf16[128,512]{1,0:T(8,128)(2,1)} %v_hbm.1), custom_call_target="tpu_custom_call" | custom-call | tf_op jit(solution)/shard_map/pallas_call | solution.py:82
  1.0 0.1 collective-permute-start.1
  1.1 1.3 %collective-permute-start.3 = (bf16[128,1024]{1,0:T(8,128)(2,1)S(1)}, bf16[128,1024]{1,0:T(8,128)(2,1)S(1)}, u32[]{:S(2)}, u32[]{:S(2)}) collective-permute-start(bf16[128,1024]{1,0:T(8,128)(2,1)S(1)} %shard_map.46.own), channel_id=1, source_target_pairs={{0,2},{1,3},{2,0},{3,1},{4,6},{5,7},{6,4},{7,5},{8,10},{9,11},{10,... | collective-permute-start | bytes 786440 | tf_op jit(solution)/shard_map/ppermute | solution.py:239
  2.4 1.1 %collective-permute-start = (bf16[128,1024]{1,0:T(8,128)(2,1)S(1)}, bf16[128,1024]{1,0:T(8,128)(2,1)S(1)}, u32[]{:S(2)}, u32[]{:S(2)}) collective-permute-start(bf16[128,1024]{1,0:T(8,128)(2,1)S(1)} %shard_map.46.own), channel_id=1, source_target_pairs={{0,1},{1,0},{2,3},{3,2},{4,5},{5,4},{6,7},{7,6},{8,9},{9,8},{10,11... | collective-permute-start | bytes 786440 | tf_op jit(solution)/shard_map/ppermute | solution.py:239
  3.5 4.8 %collective-permute-done.1.back = bf16[128,1024]{1,0:T(8,128)(2,1)S(1)} collective-permute-done((bf16[128,1024]{1,0:T(8,128)(2,1)S(1)}, bf16[128,1024]{1,0:T(8,128)(2,1)S(1)}, u32[]{:S(2)}, u32[]{:S(2)}) %collective-permute-start.1) | collective-permute-done | bytes 262176 | tf_op jit(solution)/shard_map/ppermute | solution.py:239
  8.2 1.5 %collective-permute-start.2 = (bf16[128,1024]{1,0:T(8,128)(2,1)S(1)}, bf16[128,1024]{1,0:T(8,128)(2,1)S(1)}, u32[]{:S(2)}, u32[]{:S(2)}) collective-permute-start(bf16[128,1024]{1,0:T(8,128)(2,1)S(1)} %collective-permute-done.1.back), channel_id=1, source_target_pairs={{0,1},{1,0},{2,3},{3,2},{4,5},{5,4},{6,7},{7,6},{8,9},{9,8},{10,11... | collective-permute-start | bytes 786440 | tf_op jit(solution)/shard_map/ppermute | solution.py:239
  9.8 0.1 collective-permute-start.5
  9.8 1.2 %collective-permute-start.6 = (bf16[128,1024]{1,0:T(8,128)(2,1)S(1)}, bf16[128,1024]{1,0:T(8,128)(2,1)S(1)}, u32[]{:S(2)}, u32[]{:S(2)}) collective-permute-start(bf16[128,1024]{1,0:T(8,128)(2,1)S(1)} %collective-permute-done.1.back), channel_id=1, source_target_pairs={{0,1},{1,0},{2,3},{3,2},{4,6},{5,7},{6,8},{7,9},{8,10},{9,11},{10,... | collective-permute-start | bytes 786440 | tf_op jit(solution)/shard_map/ppermute | solution.py:239
  11.1 0.0 collective-permute-done.3
  11.1 1.0 %collective-permute-start.4 = (bf16[128,1024]{1,0:T(8,128)(2,1)S(1)}, bf16[128,1024]{1,0:T(8,128)(2,1)S(1)}, u32[]{:S(2)}, u32[]{:S(2)}) collective-permute-start(bf16[128,1024]{1,0:T(8,128)(2,1)S(1)} %collective-permute-done.3), channel_id=1, source_target_pairs={{0,4},{1,5},{2,3},{3,2},{4,8},{5,9},{6,7},{7,6},{8,12},{9,13},{10,... | collective-permute-start | bytes 786440 | tf_op jit(solution)/shard_map/ppermute | solution.py:239
  12.1 0.0 collective-permute-done.sib
  12.1 0.0 collective-permute-done.2.back_sib
  12.1 4.8 %shard_map.47 = (f32[128,4096]{1,0:T(8,128)S(1)}, f32[128,4096]{1,0:T(8,128)S(1)}, f32[128,4096]{1,0:T(8,128)S(1)}, bf16[128,4096]{1,0:T(8,128)(2,1)S(1)}, s32[128,128]{1,0:T(8,128)S(1)}) custom-call(s32[16]{0:T(128)} %doc_hbm.1, bf16[128,4096]{1,0:T(8,128)(2,1)} %q_hbm.1, bf16[128,1024]{1,0:T(8,128)(2,1)S(1)} %shard_map.46.own, ...), custom_call_target="tpu_custom_call" | custom-call | flops 10737418240 | bytes 4194304 | tf_op jit(solution)/shard_map/pallas_call | solution.py:130
  16.9 0.8 %collective-permute-done.5.refs_0_ = bf16[128,1024]{1,0:T(8,128)(2,1)S(1)} collective-permute-done((bf16[128,1024]{1,0:T(8,128)(2,1)S(1)}, bf16[128,1024]{1,0:T(8,128)(2,1)S(1)}, u32[]{:S(2)}, u32[]{:S(2)}) %collective-permute-start.5) | collective-permute-done | bytes 262176 | tf_op jit(solution)/shard_map/ppermute | solution.py:239
  17.7 6.6 %collective-permute-done.6.refs_1_ = bf16[128,1024]{1,0:T(8,128)(2,1)S(1)} collective-permute-done((bf16[128,1024]{1,0:T(8,128)(2,1)S(1)}, bf16[128,1024]{1,0:T(8,128)(2,1)S(1)}, u32[]{:S(2)}, u32[]{:S(2)}) %collective-permute-start.6) | collective-permute-done | bytes 262176 | tf_op jit(solution)/shard_map/ppermute | solution.py:239
  24.3 0.0 collective-permute-done.4
  24.3 0.8 %collective-permute-start.7 = (bf16[128,1024]{1,0:T(8,128)(2,1)S(1)}, bf16[128,1024]{1,0:T(8,128)(2,1)S(1)}, u32[]{:S(2)}, u32[]{:S(2)}) collective-permute-start(bf16[128,1024]{1,0:T(8,128)(2,1)S(1)} %broadcast_select_fusion.refs_0_), channel_id=1, source_target_pairs={{0,1},{1,0},{2,3},{3,2},{4,5},{5,4},{6,7},{7,6},{8,9},{9,8},{10,11... | collective-permute-start | bytes 786440 | tf_op jit(solution)/shard_map/ppermute | solution.py:239
  25.2 0.1 collective-permute-start.8
  25.2 0.4 %collective-permute-start.9 = (bf16[128,1024]{1,0:T(8,128)(2,1)S(1)}, bf16[128,1024]{1,0:T(8,128)(2,1)S(1)}, u32[]{:S(2)}, u32[]{:S(2)}) collective-permute-start(bf16[128,1024]{1,0:T(8,128)(2,1)S(1)} %collective-permute-done.6.refs_1_), channel_id=1, source_target_pairs={{0,1},{1,0},{2,3},{3,2},{4,5},{5,4},{6,7},{7,6},{8,9},{9,8},{10,11... | collective-permute-start | bytes 786440 | tf_op jit(solution)/shard_map/ppermute | solution.py:239
  25.7 2.1 %shard_map.48 = (f32[128,4096]{1,0:T(8,128)S(1)}, f32[128,4096]{1,0:T(8,128)S(1)}, f32[128,4096]{1,0:T(8,128)S(1)}) custom-call(s32[128,128]{1,0:T(8,128)S(1)} %get-tuple-element.17.start_ref, bf16[128,4096]{1,0:T(8,128)(2,1)S(1)} %get-tuple-element.18.q_ref, bf16[128,1024]{1,0:T(8,128)(2,1)S(1)} %collective-permute-done.5.refs_0_, ...), custom_call_target="tpu_custom_call" | custom-call | flops 5368709120 | bytes 4194304 | tf_op jit(solution)/shard_map/pallas_call | solution.py:215
  27.8 0.0 collective-permute-done.7.refs_1_
  27.8 0.0 collective-permute-done.8.refs_2_
  27.8 0.0 collective-permute-done.9.refs_3_
  27.8 4.2 %shard_map.49 = bf16[128,4096]{1,0:T(8,128)(2,1)} custom-call(s32[128,128]{1,0:T(8,128)S(1)} %get-tuple-element.17.start_ref, bf16[128,4096]{1,0:T(8,128)(2,1)S(1)} %get-tuple-element.18.q_ref, bf16[128,1024]{1,0:T(8,128)(2,1)S(1)} %broadcast_select_fusion.refs_0_, bf16[128,1024]{1,0:T(8,128)(2,1)S(1)} %collective-permute-done.7.refs_1_, ...), custom_call_target="tpu_custom_call" | custom-call | flops 10737418240 | bytes 4194304 | tf_op jit(solution)/shard_map/pallas_call | solution.py:215
  (1 shorter events, 0.0 us)
Async XLA Ops:
  1.0 7.2 %collective-permute-start.1 = (bf16[128,1024]{1,0:T(8,128)(2,1)S(1)}, bf16[128,1024]{1,0:T(8,128)(2,1)S(1)}, u32[]{:S(2)}, u32[]{:S(2)}) collective-permute-start(bf16[128,1024]{1,0:T(8,128)(2,1)S(1)} %shard_map.46.own), channel_id=1, source_target_pairs={{0,4},{1,5},{2,6},{3,7},{4,8},{5,9},{6,10},{7,11},{8,12},{9,13},{1... | collective-permute-start | bytes 786440 | tf_op jit(solution)/shard_map/ppermute | solution.py:239
  1.1 10.0 %collective-permute-start.3 = (bf16[128,1024]{1,0:T(8,128)(2,1)S(1)}, bf16[128,1024]{1,0:T(8,128)(2,1)S(1)}, u32[]{:S(2)}, u32[]{:S(2)}) collective-permute-start(bf16[128,1024]{1,0:T(8,128)(2,1)S(1)} %shard_map.46.own), channel_id=1, source_target_pairs={{0,2},{1,3},{2,0},{3,1},{4,6},{5,7},{6,4},{7,5},{8,10},{9,11},{10,... | collective-permute-start | bytes 786440 | tf_op jit(solution)/shard_map/ppermute | solution.py:239
  2.4 9.7 %collective-permute-start = (bf16[128,1024]{1,0:T(8,128)(2,1)S(1)}, bf16[128,1024]{1,0:T(8,128)(2,1)S(1)}, u32[]{:S(2)}, u32[]{:S(2)}) collective-permute-start(bf16[128,1024]{1,0:T(8,128)(2,1)S(1)} %shard_map.46.own), channel_id=1, source_target_pairs={{0,1},{1,0},{2,3},{3,2},{4,5},{5,4},{6,7},{7,6},{8,9},{9,8},{10,11... | collective-permute-start | bytes 786440 | tf_op jit(solution)/shard_map/ppermute | solution.py:239
  8.2 3.9 %collective-permute-start.2 = (bf16[128,1024]{1,0:T(8,128)(2,1)S(1)}, bf16[128,1024]{1,0:T(8,128)(2,1)S(1)}, u32[]{:S(2)}, u32[]{:S(2)}) collective-permute-start(bf16[128,1024]{1,0:T(8,128)(2,1)S(1)} %collective-permute-done.1.back), channel_id=1, source_target_pairs={{0,1},{1,0},{2,3},{3,2},{4,5},{5,4},{6,7},{7,6},{8,9},{9,8},{10,11... | collective-permute-start | bytes 786440 | tf_op jit(solution)/shard_map/ppermute | solution.py:239
  9.8 7.9 %collective-permute-start.5 = (bf16[128,1024]{1,0:T(8,128)(2,1)S(1)}, bf16[128,1024]{1,0:T(8,128)(2,1)S(1)}, u32[]{:S(2)}, u32[]{:S(2)}) collective-permute-start(bf16[128,1024]{1,0:T(8,128)(2,1)S(1)} %collective-permute-done.1.back), channel_id=1, source_target_pairs={{0,1},{1,0},{2,3},{3,2},{4,8},{5,9},{6,10},{7,11},{8,12},{9,13},{1... | collective-permute-start | bytes 786440 | tf_op jit(solution)/shard_map/ppermute | solution.py:239
  9.8 14.5 %collective-permute-start.6 = (bf16[128,1024]{1,0:T(8,128)(2,1)S(1)}, bf16[128,1024]{1,0:T(8,128)(2,1)S(1)}, u32[]{:S(2)}, u32[]{:S(2)}) collective-permute-start(bf16[128,1024]{1,0:T(8,128)(2,1)S(1)} %collective-permute-done.1.back), channel_id=1, source_target_pairs={{0,1},{1,0},{2,3},{3,2},{4,6},{5,7},{6,8},{7,9},{8,10},{9,11},{10,... | collective-permute-start | bytes 786440 | tf_op jit(solution)/shard_map/ppermute | solution.py:239
  11.1 13.2 %collective-permute-start.4 = (bf16[128,1024]{1,0:T(8,128)(2,1)S(1)}, bf16[128,1024]{1,0:T(8,128)(2,1)S(1)}, u32[]{:S(2)}, u32[]{:S(2)}) collective-permute-start(bf16[128,1024]{1,0:T(8,128)(2,1)S(1)} %collective-permute-done.3), channel_id=1, source_target_pairs={{0,4},{1,5},{2,3},{3,2},{4,8},{5,9},{6,7},{7,6},{8,12},{9,13},{10,... | collective-permute-start | bytes 786440 | tf_op jit(solution)/shard_map/ppermute | solution.py:239
  24.3 3.5 %collective-permute-start.7 = (bf16[128,1024]{1,0:T(8,128)(2,1)S(1)}, bf16[128,1024]{1,0:T(8,128)(2,1)S(1)}, u32[]{:S(2)}, u32[]{:S(2)}) collective-permute-start(bf16[128,1024]{1,0:T(8,128)(2,1)S(1)} %broadcast_select_fusion.refs_0_), channel_id=1, source_target_pairs={{0,1},{1,0},{2,3},{3,2},{4,5},{5,4},{6,7},{7,6},{8,9},{9,8},{10,11... | collective-permute-start | bytes 786440 | tf_op jit(solution)/shard_map/ppermute | solution.py:239
  25.2 2.6 %collective-permute-start.8 = (bf16[128,1024]{1,0:T(8,128)(2,1)S(1)}, bf16[128,1024]{1,0:T(8,128)(2,1)S(1)}, u32[]{:S(2)}, u32[]{:S(2)}) collective-permute-start(bf16[128,1024]{1,0:T(8,128)(2,1)S(1)} %collective-permute-done.5.refs_0_), channel_id=1, source_target_pairs={{0,1},{1,0},{2,3},{3,2},{4,5},{5,4},{6,7},{7,6},{8,9},{9,8},{10,11... | collective-permute-start | bytes 786440 | tf_op jit(solution)/shard_map/ppermute | solution.py:239
  25.2 2.6 %collective-permute-start.9 = (bf16[128,1024]{1,0:T(8,128)(2,1)S(1)}, bf16[128,1024]{1,0:T(8,128)(2,1)S(1)}, u32[]{:S(2)}, u32[]{:S(2)}) collective-permute-start(bf16[128,1024]{1,0:T(8,128)(2,1)S(1)} %collective-permute-done.6.refs_1_), channel_id=1, source_target_pairs={{0,1},{1,0},{2,3},{3,2},{4,5},{5,4},{6,7},{7,6},{8,9},{9,8},{10,11... | collective-permute-start | bytes 786440 | tf_op jit(solution)/shard_map/ppermute | solution.py:239

commit v5 on v4

--- a/solution.py
+++ b/solution.py
@@ -163,7 +163,7 @@
             rest[0][:, at], rest[1][:, at], rest[2][:, at] = new
 
     def out_copy(j):
-        at = head_columns(j * GROUP, GROUP)
+        at = head_columns(j * (GROUP // 2), GROUP // 2)
         return pltpu.make_async_copy(out_ref.at[:, at], out_hbm.at[:, at], sems.at[j])
 
     def update(used):
@@ -183,26 +183,25 @@
                     at = head_columns(j * GROUP + g)
                     emit(at, *(x[:, at] for x in state))
             if last:
-                out_copy(j).start()
+                out_copy(2 * j).start()
+                out_copy(2 * j + 1).start()
 
     every = list(range(n_blocks))
-    near = [b for b in every if places[b][0] == min(places)[0]]
-    further = [offset for offset, _ in places if offset > min(places)[0]]
+    nearest, furthest = (pick(offset for offset, _ in places) for pick in (min, max))
+    near = [b for b in every if places[b][0] < furthest]
 
     def seen(offset):
         return (2 * (chip - offset) + 2) * rows > first_start
 
-    seen_near = seen(min(places)[0])
-    pl.when(jnp.logical_not(seen_near))(lambda: update([]))
-    if further and len(near) > 1:
-        seen_all = seen(min(further))
-        pl.when(seen_near & jnp.logical_not(seen_all))(lambda: update(near))
-        pl.when(seen_all)(lambda: update(every))
+    pl.when(jnp.logical_not(seen(nearest)))(lambda: update([]))
+    if near and len(near) % 2 == 0:
+        pl.when(seen(nearest) & jnp.logical_not(seen(furthest)))(lambda: update(near))
+        pl.when(seen(furthest))(lambda: update(every))
     else:
-        pl.when(seen_near)(lambda: update(every))
+        pl.when(seen(nearest))(lambda: update(every))
 
     if last:
-        for j in range(KV_HEADS):
+        for j in range(2 * KV_HEADS):
             out_copy(j).wait()
 
 
@@ -211,7 +210,7 @@
     wide = jax.ShapeDtypeStruct(queries.shape, jnp.float32)
     scratch = []
     if last:
-        scratch = [pltpu.VMEM(queries.shape, queries.dtype), pltpu.SemaphoreType.DMA((KV_HEADS,))]
+        scratch = [pltpu.VMEM(queries.shape, queries.dtype), pltpu.SemaphoreType.DMA((2 * KV_HEADS,))]
     return pl.pallas_call(
         functools.partial(next_kernel, last, places),
         out_shape=jax.ShapeDtypeStruct(queries.shape, queries.dtype) if last else (wide,) * 3,
@@ -259,13 +258,20 @@
     *state, q, start = attend_first(doc_lengths, queries, *pair(own), *pair(back))
     back_beside, beside, far = after((back_beside, beside, far), state[0])
     even = lax.axis_index("ctx") // 2 % 2 == 0
-    blocks, places = pair(jnp.where(even, back_beside, beside)), ((1, 0), (1, 1))
+    across = jnp.where(even, back_beside, beside)
+    blocks, places = (across,), (1,)
     for z in range(2, reach + 1):
-        here, other = far, tuple(swap(block, 1) for block in far)
+        here, there = far
         if z < reach:
-            far = after((onward(far[0], 4, z + 1), onward(far[0], 2, z + 1)), state[0])
-        state = attend_next(start, q, here, ((2 * z, 0), (2 * z - 1, 0)), state)
-        blocks, places = blocks + other, places + ((2 * z, 1), (2 * z - 1, 1))
+            far = after((onward(here, 4, z + 1), onward(here, 2, z + 1)), state[0])
+        blocks, places = (there,) + blocks, (2 * z - 1,) + places
+        other = tuple(swap(block, 1) for block in blocks)
+        if len(blocks) == 2:
+            state = attend_next(start, q, blocks, tuple((offset, 0) for offset in places), state)
+            blocks, places = (), ()
+        blocks = blocks + other + pair(here)
+        places = tuple((offset, 0) for offset in places) + tuple((offset, 1) for offset in (2 * z - 1, 1)[: len(other)])
+        places = places + ((2 * z, 0), (2 * z, 1))
         if z < reach:
             state = attend_next(start, q, blocks, places, state)
             blocks, places = (), ()

time: 32.3 us -> 32 us (level)
  the two profiles are of different devices: /device:TPU:27 before, /device:TPU:1 now
where the time goes in v5:
time: 32 us; the launch traced here: 31.6 us
  waiting for transfers between devices  13.8 us (43%)
  starting transfers between devices  9.53 us (30%)
  Pallas kernels  8.03 us (25%)
    ppermute x10, waiting for transfers between devices, permute(): return lax.ppermute(block, 'ctx', [(i, target(i)) for i in range(n)])  13.8 us
    ppermute x10, starting transfers between devices, permute(): return lax.ppermute(block, 'ctx', [(i, target(i)) for i in range(n)])  9.53 us
    pallas_call x1, Pallas kernels, attend_first(): pl.pallas_call(first_kernel, out_shape=(wide, wide, wide, queries, jax.Sh...  4.83 us
    pallas_call x2, Pallas kernels, attend_next(): pl.pallas_call(functools.partial(next_kernel, last, places), out_shape=ja...  2.21 us
    pallas_call x1, Pallas kernels, pack(): pl.pallas_call(pack_kernel, out_shape=jax.ShapeDtypeStruct((rows, 2 * hal...  0.98 us
  transfers between devices with their start and end apart: 10, of which 4 were waited for; matrix products, arithmetic and copies ran while one was open for 0% of the time, Pallas kernels for 18%

profile of v5, /device:TPU:1, one launch (start us, length us, event | category | flops | bytes accessed | tf_op | source)
XLA Modules:
  0.0 31.6 jit_solution(11117096907975394582)
XLA Ops:
  0.0 1.0 %shard_map.46.own = bf16[128,1024]{1,0:T(8,128)(2,1)S(1)} custom-call(bf16[128,512]{1,0:T(8,128)(2,1)} %k_hbm.1, bf16[128,512]{1,0:T(8,128)(2,1)} %v_hbm.1), custom_call_target="tpu_custom_call" | custom-call | tf_op jit(solution)/shard_map/pallas_call | solution.py:82
  1.0 2.2 %collective-permute-start.1 = (bf16[128,1024]{1,0:T(8,128)(2,1)S(1)}, bf16[128,1024]{1,0:T(8,128)(2,1)S(1)}, u32[]{:S(2)}, u32[]{:S(2)}) collective-permute-start(bf16[128,1024]{1,0:T(8,128)(2,1)S(1)} %shard_map.46.own), channel_id=1, source_target_pairs={{0,4},{1,5},{2,6},{3,7},{4,8},{5,9},{6,10},{7,11},{8,12},{9,13},{1... | collective-permute-start | bytes 786440 | tf_op jit(solution)/shard_map/ppermute | solution.py:238
  3.2 1.2 %collective-permute-start.3 = (bf16[128,1024]{1,0:T(8,128)(2,1)S(1)}, bf16[128,1024]{1,0:T(8,128)(2,1)S(1)}, u32[]{:S(2)}, u32[]{:S(2)}) collective-permute-start(bf16[128,1024]{1,0:T(8,128)(2,1)S(1)} %shard_map.46.own), channel_id=1, source_target_pairs={{0,2},{1,3},{2,0},{3,1},{4,6},{5,7},{6,4},{7,5},{8,10},{9,11},{10,... | collective-permute-start | bytes 786440 | tf_op jit(solution)/shard_map/ppermute | solution.py:238
  4.4 1.2 %collective-permute-start = (bf16[128,1024]{1,0:T(8,128)(2,1)S(1)}, bf16[128,1024]{1,0:T(8,128)(2,1)S(1)}, u32[]{:S(2)}, u32[]{:S(2)}) collective-permute-start(bf16[128,1024]{1,0:T(8,128)(2,1)S(1)} %shard_map.46.own), channel_id=1, source_target_pairs={{0,1},{1,0},{2,3},{3,2},{4,5},{5,4},{6,7},{7,6},{8,9},{9,8},{10,11... | collective-permute-start | bytes 786440 | tf_op jit(solution)/shard_map/ppermute | solution.py:238
  5.6 5.6 %collective-permute-done.1.back = bf16[128,1024]{1,0:T(8,128)(2,1)S(1)} collective-permute-done((bf16[128,1024]{1,0:T(8,128)(2,1)S(1)}, bf16[128,1024]{1,0:T(8,128)(2,1)S(1)}, u32[]{:S(2)}, u32[]{:S(2)}) %collective-permute-start.1) | collective-permute-done | bytes 262176 | tf_op jit(solution)/shard_map/ppermute | solution.py:238
  11.2 1.2 %collective-permute-start.2 = (bf16[128,1024]{1,0:T(8,128)(2,1)S(1)}, bf16[128,1024]{1,0:T(8,128)(2,1)S(1)}, u32[]{:S(2)}, u32[]{:S(2)}) collective-permute-start(bf16[128,1024]{1,0:T(8,128)(2,1)S(1)} %collective-permute-done.1.back), channel_id=1, source_target_pairs={{0,1},{1,0},{2,3},{3,2},{4,5},{5,4},{6,7},{7,6},{8,9},{9,8},{10,11... | collective-permute-start | bytes 786440 | tf_op jit(solution)/shard_map/ppermute | solution.py:238
  12.5 0.0 collective-permute-start.6
  12.5 0.5 %collective-permute-start.5 = (bf16[128,1024]{1,0:T(8,128)(2,1)S(1)}, bf16[128,1024]{1,0:T(8,128)(2,1)S(1)}, u32[]{:S(2)}, u32[]{:S(2)}) collective-permute-start(bf16[128,1024]{1,0:T(8,128)(2,1)S(1)} %collective-permute-done.1.back), channel_id=1, source_target_pairs={{0,1},{1,0},{2,3},{3,2},{4,8},{5,9},{6,10},{7,11},{8,12},{9,13},{1... | collective-permute-start | bytes 786440 | tf_op jit(solution)/shard_map/ppermute | solution.py:238
  13.0 0.0 collective-permute-done.3
  13.0 1.5 %collective-permute-start.4 = (bf16[128,1024]{1,0:T(8,128)(2,1)S(1)}, bf16[128,1024]{1,0:T(8,128)(2,1)S(1)}, u32[]{:S(2)}, u32[]{:S(2)}) collective-permute-start(bf16[128,1024]{1,0:T(8,128)(2,1)S(1)} %collective-permute-done.3), channel_id=1, source_target_pairs={{0,4},{1,5},{2,3},{3,2},{4,8},{5,9},{6,7},{7,6},{8,12},{9,13},{10,... | collective-permute-start | bytes 786440 | tf_op jit(solution)/shard_map/ppermute | solution.py:238
  14.4 0.0 collective-permute-done.sib
  14.4 0.0 collective-permute-done.2.back_sib
  14.4 4.8 %shard_map.47 = (f32[128,4096]{1,0:T(8,128)S(1)}, f32[128,4096]{1,0:T(8,128)S(1)}, f32[128,4096]{1,0:T(8,128)S(1)}, bf16[128,4096]{1,0:T(8,128)(2,1)S(1)}, s32[128,128]{1,0:T(8,128)S(1)}) custom-call(s32[16]{0:T(128)} %doc_hbm.1, bf16[128,4096]{1,0:T(8,128)(2,1)} %q_hbm.1, bf16[128,1024]{1,0:T(8,128)(2,1)S(1)} %shard_map.46.own, ...), custom_call_target="tpu_custom_call" | custom-call | flops 10737418240 | bytes 4194304 | tf_op jit(solution)/shard_map/pallas_call | solution.py:130
  19.3 7.7 %collective-permute-done.4 = bf16[128,1024]{1,0:T(8,128)(2,1)S(1)} collective-permute-done((bf16[128,1024]{1,0:T(8,128)(2,1)S(1)}, bf16[128,1024]{1,0:T(8,128)(2,1)S(1)}, u32[]{:S(2)}, u32[]{:S(2)}) %collective-permute-start.4) | collective-permute-done | bytes 262176 | tf_op jit(solution)/shard_map/ppermute | solution.py:238
  27.0 0.0 collective-permute-done.6.refs_0_
  27.0 0.0 collective-permute-done.5.refs_2_
  27.0 1.2 %collective-permute-start.8 = (bf16[128,1024]{1,0:T(8,128)(2,1)S(1)}, bf16[128,1024]{1,0:T(8,128)(2,1)S(1)}, u32[]{:S(2)}, u32[]{:S(2)}) collective-permute-start(bf16[128,1024]{1,0:T(8,128)(2,1)S(1)} %broadcast_select_fusion.refs_1_), channel_id=1, source_target_pairs={{0,1},{1,0},{2,3},{3,2},{4,5},{5,4},{6,7},{7,6},{8,9},{9,8},{10,11... | collective-permute-start | bytes 786440 | tf_op jit(solution)/shard_map/ppermute | solution.py:238
  28.2 0.1 collective-permute-start.7
  28.3 0.4 %collective-permute-start.9 = (bf16[128,1024]{1,0:T(8,128)(2,1)S(1)}, bf16[128,1024]{1,0:T(8,128)(2,1)S(1)}, u32[]{:S(2)}, u32[]{:S(2)}) collective-permute-start(bf16[128,1024]{1,0:T(8,128)(2,1)S(1)} %collective-permute-done.5.refs_2_), channel_id=1, source_target_pairs={{0,1},{1,0},{2,3},{3,2},{4,5},{5,4},{6,7},{7,6},{8,9},{9,8},{10,11... | collective-permute-start | bytes 786440 | tf_op jit(solution)/shard_map/ppermute | solution.py:238
  28.7 0.9 %shard_map.48 = (f32[128,4096]{1,0:T(8,128)S(1)}, f32[128,4096]{1,0:T(8,128)S(1)}, f32[128,4096]{1,0:T(8,128)S(1)}) custom-call(s32[128,128]{1,0:T(8,128)S(1)} %get-tuple-element.17.start_ref, bf16[128,4096]{1,0:T(8,128)(2,1)S(1)} %get-tuple-element.18.q_ref, bf16[128,1024]{1,0:T(8,128)(2,1)S(1)} %collective-permute-done.6.refs_0_, ...), custom_call_target="tpu_custom_call" | custom-call | flops 5368709120 | bytes 4194304 | tf_op jit(solution)/shard_map/pallas_call | solution.py:214
  29.6 0.0 collective-permute-done.8.refs_1_
  29.6 0.1 collective-permute-done.7.refs_0_
  29.7 0.4 %collective-permute-done.9.refs_3_ = bf16[128,1024]{1,0:T(8,128)(2,1)S(1)} collective-permute-done((bf16[128,1024]{1,0:T(8,128)(2,1)S(1)}, bf16[128,1024]{1,0:T(8,128)(2,1)S(1)}, u32[]{:S(2)}, u32[]{:S(2)}) %collective-permute-start.9) | collective-permute-done | bytes 262176 | tf_op jit(solution)/shard_map/ppermute | solution.py:238
  30.1 1.3 %shard_map.49 = bf16[128,4096]{1,0:T(8,128)(2,1)} custom-call(s32[128,128]{1,0:T(8,128)S(1)} %get-tuple-element.17.start_ref, bf16[128,4096]{1,0:T(8,128)(2,1)S(1)} %get-tuple-element.18.q_ref, bf16[128,1024]{1,0:T(8,128)(2,1)S(1)} %collective-permute-done.7.refs_0_, bf16[128,1024]{1,0:T(8,128)(2,1)S(1)} %collective-permute-done.8.refs_1_, ...), custom_call_target="tpu_custom_call" | custom-call | flops 10737418240 | bytes 4194304 | tf_op jit(solution)/shard_map/pallas_call | solution.py:214
  (1 shorter events, 0.0 us)
Async XLA Ops:
  1.0 10.2 %collective-permute-start.1 = (bf16[128,1024]{1,0:T(8,128)(2,1)S(1)}, bf16[128,1024]{1,0:T(8,128)(2,1)S(1)}, u32[]{:S(2)}, u32[]{:S(2)}) collective-permute-start(bf16[128,1024]{1,0:T(8,128)(2,1)S(1)} %shard_map.46.own), channel_id=1, source_target_pairs={{0,4},{1,5},{2,6},{3,7},{4,8},{5,9},{6,10},{7,11},{8,12},{9,13},{1... | collective-permute-start | bytes 786440 | tf_op jit(solution)/shard_map/ppermute | solution.py:238
  3.2 9.8 %collective-permute-start.3 = (bf16[128,1024]{1,0:T(8,128)(2,1)S(1)}, bf16[128,1024]{1,0:T(8,128)(2,1)S(1)}, u32[]{:S(2)}, u32[]{:S(2)}) collective-permute-start(bf16[128,1024]{1,0:T(8,128)(2,1)S(1)} %shard_map.46.own), channel_id=1, source_target_pairs={{0,2},{1,3},{2,0},{3,1},{4,6},{5,7},{6,4},{7,5},{8,10},{9,11},{10,... | collective-permute-start | bytes 786440 | tf_op jit(solution)/shard_map/ppermute | solution.py:238
  4.4 10.0 %collective-permute-start = (bf16[128,1024]{1,0:T(8,128)(2,1)S(1)}, bf16[128,1024]{1,0:T(8,128)(2,1)S(1)}, u32[]{:S(2)}, u32[]{:S(2)}) collective-permute-start(bf16[128,1024]{1,0:T(8,128)(2,1)S(1)} %shard_map.46.own), channel_id=1, source_target_pairs={{0,1},{1,0},{2,3},{3,2},{4,5},{5,4},{6,7},{7,6},{8,9},{9,8},{10,11... | collective-permute-start | bytes 786440 | tf_op jit(solution)/shard_map/ppermute | solution.py:238
  11.2 3.2 %collective-permute-start.2 = (bf16[128,1024]{1,0:T(8,128)(2,1)S(1)}, bf16[128,1024]{1,0:T(8,128)(2,1)S(1)}, u32[]{:S(2)}, u32[]{:S(2)}) collective-permute-start(bf16[128,1024]{1,0:T(8,128)(2,1)S(1)} %collective-permute-done.1.back), channel_id=1, source_target_pairs={{0,1},{1,0},{2,3},{3,2},{4,5},{5,4},{6,7},{7,6},{8,9},{9,8},{10,11... | collective-permute-start | bytes 786440 | tf_op jit(solution)/shard_map/ppermute | solution.py:238
  12.5 14.5 %collective-permute-start.6 = (bf16[128,1024]{1,0:T(8,128)(2,1)S(1)}, bf16[128,1024]{1,0:T(8,128)(2,1)S(1)}, u32[]{:S(2)}, u32[]{:S(2)}) collective-permute-start(bf16[128,1024]{1,0:T(8,128)(2,1)S(1)} %collective-permute-done.1.back), channel_id=1, source_target_pairs={{0,1},{1,0},{2,3},{3,2},{4,6},{5,7},{6,8},{7,9},{8,10},{9,11},{10,... | collective-permute-start | bytes 786440 | tf_op jit(solution)/shard_map/ppermute | solution.py:238
  12.5 14.5 %collective-permute-start.5 = (bf16[128,1024]{1,0:T(8,128)(2,1)S(1)}, bf16[128,1024]{1,0:T(8,128)(2,1)S(1)}, u32[]{:S(2)}, u32[]{:S(2)}) collective-permute-start(bf16[128,1024]{1,0:T(8,128)(2,1)S(1)} %collective-permute-done.1.back), channel_id=1, source_target_pairs={{0,1},{1,0},{2,3},{3,2},{4,8},{5,9},{6,10},{7,11},{8,12},{9,13},{1... | collective-permute-start | bytes 786440 | tf_op jit(solution)/shard_map/ppermute | solution.py:238
  13.0 14.0 %collective-permute-start.4 = (bf16[128,1024]{1,0:T(8,128)(2,1)S(1)}, bf16[128,1024]{1,0:T(8,128)(2,1)S(1)}, u32[]{:S(2)}, u32[]{:S(2)}) collective-permute-start(bf16[128,1024]{1,0:T(8,128)(2,1)S(1)} %collective-permute-done.3), channel_id=1, source_target_pairs={{0,4},{1,5},{2,3},{3,2},{4,8},{5,9},{6,7},{7,6},{8,12},{9,13},{10,... | collective-permute-start | bytes 786440 | tf_op jit(solution)/shard_map/ppermute | solution.py:238
  27.0 2.6 %collective-permute-start.8 = (bf16[128,1024]{1,0:T(8,128)(2,1)S(1)}, bf16[128,1024]{1,0:T(8,128)(2,1)S(1)}, u32[]{:S(2)}, u32[]{:S(2)}) collective-permute-start(bf16[128,1024]{1,0:T(8,128)(2,1)S(1)} %broadcast_select_fusion.refs_1_), channel_id=1, source_target_pairs={{0,1},{1,0},{2,3},{3,2},{4,5},{5,4},{6,7},{7,6},{8,9},{9,8},{10,11... | collective-permute-start | bytes 786440 | tf_op jit(solution)/shard_map/ppermute | solution.py:238
  28.2 1.5 %collective-permute-start.7 = (bf16[128,1024]{1,0:T(8,128)(2,1)S(1)}, bf16[128,1024]{1,0:T(8,128)(2,1)S(1)}, u32[]{:S(2)}, u32[]{:S(2)}) collective-permute-start(bf16[128,1024]{1,0:T(8,128)(2,1)S(1)} %collective-permute-done.6.refs_0_), channel_id=1, source_target_pairs={{0,1},{1,0},{2,3},{3,2},{4,5},{5,4},{6,7},{7,6},{8,9},{9,8},{10,11... | collective-permute-start | bytes 786440 | tf_op jit(solution)/shard_map/ppermute | solution.py:238
  28.3 1.8 %collective-permute-start.9 = (bf16[128,1024]{1,0:T(8,128)(2,1)S(1)}, bf16[128,1024]{1,0:T(8,128)(2,1)S(1)}, u32[]{:S(2)}, u32[]{:S(2)}) collective-permute-start(bf16[128,1024]{1,0:T(8,128)(2,1)S(1)} %collective-permute-done.5.refs_2_), channel_id=1, source_target_pairs={{0,1},{1,0},{2,3},{3,2},{4,5},{5,4},{6,7},{7,6},{8,9},{9,8},{10,11... | collective-permute-start | bytes 786440 | tf_op jit(solution)/shard_map/ppermute | solution.py:238

commit v6 on v5

--- a/solution.py
+++ b/solution.py
@@ -241,7 +241,7 @@
         return permute(block, lambda i: i ^ bit)
 
     def onward(block, step, hop):
-        fixed = 4 * (hop - 1)
+        fixed = 4 * (hop - 1) - 2 * (step % 4)
         return permute(block, lambda i: i ^ 1 if i < fixed else fixed + (i - fixed + step) % (n - fixed))
 
     def after(block, other):
@@ -254,7 +254,7 @@
     beside = swap(own, 2)
     back = onward(own, 4, 1)
     back_beside = permute(beside, lambda i: i ^ 1 if i // 2 % 2 else (i + 4) % n)
-    far = (onward(back, 4, 2), onward(back, 2, 2)) if reach > 1 else ()
+    far = (onward(after(back, swap(beside, 1)), 4, 2), onward(back, 2, 2)) if reach > 1 else ()
     *state, q, start = attend_first(doc_lengths, queries, *pair(own), *pair(back))
     back_beside, beside, far = after((back_beside, beside, far), state[0])
     even = lax.axis_index("ctx") // 2 % 2 == 0

time: 32 us -> 31.7 us (level)
  transfers between devices with their start and end apart: 10 -> 10, of which waited for: 4 -> 5; matrix products, arithmetic and copies ran while one was open for 0% -> 0% of each run, Pallas kernels for 18% -> 18%
where the time goes in v6:
time: 31.7 us; the launch traced here: 31.3 us
  waiting for transfers between devices  13.8 us (44%)
  starting transfers between devices  9.21 us (29%)
  Pallas kernels  8.03 us (25%)
    ppermute x10, waiting for transfers between devices, permute(): return lax.ppermute(block, 'ctx', [(i, target(i)) for i in range(n)])  13.8 us
    ppermute x10, starting transfers between devices, permute(): return lax.ppermute(block, 'ctx', [(i, target(i)) for i in range(n)])  9.21 us
    pallas_call x1, Pallas kernels, attend_first(): pl.pallas_call(first_kernel, out_shape=(wide, wide, wide, queries, jax.Sh...  4.83 us
    pallas_call x2, Pallas kernels, attend_next(): pl.pallas_call(functools.partial(next_kernel, last, places), out_shape=ja...  2.21 us
    pallas_call x1, Pallas kernels, pack(): pl.pallas_call(pack_kernel, out_shape=jax.ShapeDtypeStruct((rows, 2 * hal...  0.98 us
  transfers between devices with their start and end apart: 10, of which 5 were waited for; matrix products, arithmetic and copies ran while one was open for 0% of the time, Pallas kernels for 18%

profile of v6, /device:TPU:1, one launch (start us, length us, event | category | flops | bytes accessed | tf_op | source)
XLA Modules:
  0.0 31.3 jit_solution(7940321054263174168)
XLA Ops:
  0.0 1.0 %shard_map.46.own = bf16[128,1024]{1,0:T(8,128)(2,1)S(1)} custom-call(bf16[128,512]{1,0:T(8,128)(2,1)} %k_hbm.1, bf16[128,512]{1,0:T(8,128)(2,1)} %v_hbm.1), custom_call_target="tpu_custom_call" | custom-call | tf_op jit(solution)/shard_map/pallas_call | solution.py:82
  1.0 2.2 %collective-permute-start.1 = (bf16[128,1024]{1,0:T(8,128)(2,1)S(1)}, bf16[128,1024]{1,0:T(8,128)(2,1)S(1)}, u32[]{:S(2)}, u32[]{:S(2)}) collective-permute-start(bf16[128,1024]{1,0:T(8,128)(2,1)S(1)} %shard_map.46.own), channel_id=1, source_target_pairs={{0,4},{1,5},{2,6},{3,7},{4,8},{5,9},{6,10},{7,11},{8,12},{9,13},{1... | collective-permute-start | bytes 786440 | tf_op jit(solution)/shard_map/ppermute | solution.py:238
  3.2 1.2 %collective-permute-start.3 = (bf16[128,1024]{1,0:T(8,128)(2,1)S(1)}, bf16[128,1024]{1,0:T(8,128)(2,1)S(1)}, u32[]{:S(2)}, u32[]{:S(2)}) collective-permute-start(bf16[128,1024]{1,0:T(8,128)(2,1)S(1)} %shard_map.46.own), channel_id=1, source_target_pairs={{0,2},{1,3},{2,0},{3,1},{4,6},{5,7},{6,4},{7,5},{8,10},{9,11},{10,... | collective-permute-start | bytes 786440 | tf_op jit(solution)/shard_map/ppermute | solution.py:238
  4.4 1.2 %collective-permute-start = (bf16[128,1024]{1,0:T(8,128)(2,1)S(1)}, bf16[128,1024]{1,0:T(8,128)(2,1)S(1)}, u32[]{:S(2)}, u32[]{:S(2)}) collective-permute-start(bf16[128,1024]{1,0:T(8,128)(2,1)S(1)} %shard_map.46.own), channel_id=1, source_target_pairs={{0,1},{1,0},{2,3},{3,2},{4,5},{5,4},{6,7},{7,6},{8,9},{9,8},{10,11... | collective-permute-start | bytes 786440 | tf_op jit(solution)/shard_map/ppermute | solution.py:238
  5.6 5.6 %collective-permute-done.1.back = bf16[128,1024]{1,0:T(8,128)(2,1)S(1)} collective-permute-done((bf16[128,1024]{1,0:T(8,128)(2,1)S(1)}, bf16[128,1024]{1,0:T(8,128)(2,1)S(1)}, u32[]{:S(2)}, u32[]{:S(2)}) %collective-permute-start.1) | collective-permute-done | bytes 262176 | tf_op jit(solution)/shard_map/ppermute | solution.py:238
  11.2 1.2 %collective-permute-start.2 = (bf16[128,1024]{1,0:T(8,128)(2,1)S(1)}, bf16[128,1024]{1,0:T(8,128)(2,1)S(1)}, u32[]{:S(2)}, u32[]{:S(2)}) collective-permute-start(bf16[128,1024]{1,0:T(8,128)(2,1)S(1)} %collective-permute-done.1.back), channel_id=1, source_target_pairs={{0,1},{1,0},{2,3},{3,2},{4,5},{5,4},{6,7},{7,6},{8,9},{9,8},{10,11... | collective-permute-start | bytes 786440 | tf_op jit(solution)/shard_map/ppermute | solution.py:238
  12.5 0.0 collective-permute-start.5
  12.5 1.2 %collective-permute-start.6 = (bf16[128,1024]{1,0:T(8,128)(2,1)S(1)}, bf16[128,1024]{1,0:T(8,128)(2,1)S(1)}, u32[]{:S(2)}, u32[]{:S(2)}) collective-permute-start(bf16[128,1024]{1,0:T(8,128)(2,1)S(1)} %collective-permute-done.1.back), channel_id=1, source_target_pairs={{0,2},{1,3},{2,4},{3,5},{4,6},{5,7},{6,8},{7,9},{8,10},{9,11},{10,... | collective-permute-start | bytes 786440 | tf_op jit(solution)/shard_map/ppermute | solution.py:238
  13.7 0.0 collective-permute-done.3
  13.7 0.7 %collective-permute-start.4 = (bf16[128,1024]{1,0:T(8,128)(2,1)S(1)}, bf16[128,1024]{1,0:T(8,128)(2,1)S(1)}, u32[]{:S(2)}, u32[]{:S(2)}) collective-permute-start(bf16[128,1024]{1,0:T(8,128)(2,1)S(1)} %collective-permute-done.3), channel_id=1, source_target_pairs={{0,4},{1,5},{2,3},{3,2},{4,8},{5,9},{6,7},{7,6},{8,12},{9,13},{10,... | collective-permute-start | bytes 786440 | tf_op jit(solution)/shard_map/ppermute | solution.py:238
  14.4 0.0 collective-permute-done.sib
  14.4 0.0 collective-permute-done.2.back_sib
  14.4 4.8 %shard_map.47 = (f32[128,4096]{1,0:T(8,128)S(1)}, f32[128,4096]{1,0:T(8,128)S(1)}, f32[128,4096]{1,0:T(8,128)S(1)}, bf16[128,4096]{1,0:T(8,128)(2,1)S(1)}, s32[128,128]{1,0:T(8,128)S(1)}) custom-call(s32[16]{0:T(128)} %doc_hbm.1, bf16[128,4096]{1,0:T(8,128)(2,1)} %q_hbm.1, bf16[128,1024]{1,0:T(8,128)(2,1)S(1)} %shard_map.46.own, ...), custom_call_target="tpu_custom_call" | custom-call | flops 10737418240 | bytes 4194304 | tf_op jit(solution)/shard_map/pallas_call | solution.py:130
  19.3 6.8 %collective-permute-done.4 = bf16[128,1024]{1,0:T(8,128)(2,1)S(1)} collective-permute-done((bf16[128,1024]{1,0:T(8,128)(2,1)S(1)}, bf16[128,1024]{1,0:T(8,128)(2,1)S(1)}, u32[]{:S(2)}, u32[]{:S(2)}) %collective-permute-start.4) | collective-permute-done | bytes 262176 | tf_op jit(solution)/shard_map/ppermute | solution.py:238
  26.1 0.0 collective-permute-done.5.refs_2_
  26.1 1.0 %collective-permute-done.6.refs_0_ = bf16[128,1024]{1,0:T(8,128)(2,1)S(1)} collective-permute-done((bf16[128,1024]{1,0:T(8,128)(2,1)S(1)}, bf16[128,1024]{1,0:T(8,128)(2,1)S(1)}, u32[]{:S(2)}, u32[]{:S(2)}) %collective-permute-start.6) | collective-permute-done | bytes 262176 | tf_op jit(solution)/shard_map/ppermute | solution.py:238
  27.1 0.8 %collective-permute-start.8 = (bf16[128,1024]{1,0:T(8,128)(2,1)S(1)}, bf16[128,1024]{1,0:T(8,128)(2,1)S(1)}, u32[]{:S(2)}, u32[]{:S(2)}) collective-permute-start(bf16[128,1024]{1,0:T(8,128)(2,1)S(1)} %broadcast_select_fusion.refs_1_), channel_id=1, source_target_pairs={{0,1},{1,0},{2,3},{3,2},{4,5},{5,4},{6,7},{7,6},{8,9},{9,8},{10,11... | collective-permute-start | bytes 786440 | tf_op jit(solution)/shard_map/ppermute | solution.py:238
  27.9 0.1 collective-permute-start.7
  28.0 0.4 %collective-permute-start.9 = (bf16[128,1024]{1,0:T(8,128)(2,1)S(1)}, bf16[128,1024]{1,0:T(8,128)(2,1)S(1)}, u32[]{:S(2)}, u32[]{:S(2)}) collective-permute-start(bf16[128,1024]{1,0:T(8,128)(2,1)S(1)} %collective-permute-done.5.refs_2_), channel_id=1, source_target_pairs={{0,1},{1,0},{2,3},{3,2},{4,5},{5,4},{6,7},{7,6},{8,9},{9,8},{10,11... | collective-permute-start | bytes 786440 | tf_op jit(solution)/shard_map/ppermute | solution.py:238
  28.4 0.9 %shard_map.48 = (f32[128,4096]{1,0:T(8,128)S(1)}, f32[128,4096]{1,0:T(8,128)S(1)}, f32[128,4096]{1,0:T(8,128)S(1)}) custom-call(s32[128,128]{1,0:T(8,128)S(1)} %get-tuple-element.17.start_ref, bf16[128,4096]{1,0:T(8,128)(2,1)S(1)} %get-tuple-element.18.q_ref, bf16[128,1024]{1,0:T(8,128)(2,1)S(1)} %collective-permute-done.6.refs_0_, ...), custom_call_target="tpu_custom_call" | custom-call | flops 5368709120 | bytes 4194304 | tf_op jit(solution)/shard_map/pallas_call | solution.py:214
  29.3 0.0 collective-permute-done.8.refs_1_
  29.3 0.1 collective-permute-done.7.refs_0_
  29.4 0.4 %collective-permute-done.9.refs_3_ = bf16[128,1024]{1,0:T(8,128)(2,1)S(1)} collective-permute-done((bf16[128,1024]{1,0:T(8,128)(2,1)S(1)}, bf16[128,1024]{1,0:T(8,128)(2,1)S(1)}, u32[]{:S(2)}, u32[]{:S(2)}) %collective-permute-start.9) | collective-permute-done | bytes 262176 | tf_op jit(solution)/shard_map/ppermute | solution.py:238
  29.8 1.3 %shard_map.49 = bf16[128,4096]{1,0:T(8,128)(2,1)} custom-call(s32[128,128]{1,0:T(8,128)S(1)} %get-tuple-element.17.start_ref, bf16[128,4096]{1,0:T(8,128)(2,1)S(1)} %get-tuple-element.18.q_ref, bf16[128,1024]{1,0:T(8,128)(2,1)S(1)} %collective-permute-done.7.refs_0_, bf16[128,1024]{1,0:T(8,128)(2,1)S(1)} %collective-permute-done.8.refs_1_, ...), custom_call_target="tpu_custom_call" | custom-call | flops 10737418240 | bytes 4194304 | tf_op jit(solution)/shard_map/pallas_call | solution.py:214
  (1 shorter events, 0.0 us)
Async XLA Ops:
  1.0 10.2 %collective-permute-start.1 = (bf16[128,1024]{1,0:T(8,128)(2,1)S(1)}, bf16[128,1024]{1,0:T(8,128)(2,1)S(1)}, u32[]{:S(2)}, u32[]{:S(2)}) collective-permute-start(bf16[128,1024]{1,0:T(8,128)(2,1)S(1)} %shard_map.46.own), channel_id=1, source_target_pairs={{0,4},{1,5},{2,6},{3,7},{4,8},{5,9},{6,10},{7,11},{8,12},{9,13},{1... | collective-permute-start | bytes 786440 | tf_op jit(solution)/shard_map/ppermute | solution.py:238
  3.2 10.5 %collective-permute-start.3 = (bf16[128,1024]{1,0:T(8,128)(2,1)S(1)}, bf16[128,1024]{1,0:T(8,128)(2,1)S(1)}, u32[]{:S(2)}, u32[]{:S(2)}) collective-permute-start(bf16[128,1024]{1,0:T(8,128)(2,1)S(1)} %shard_map.46.own), channel_id=1, source_target_pairs={{0,2},{1,3},{2,0},{3,1},{4,6},{5,7},{6,4},{7,5},{8,10},{9,11},{10,... | collective-permute-start | bytes 786440 | tf_op jit(solution)/shard_map/ppermute | solution.py:238
  4.4 10.0 %collective-permute-start = (bf16[128,1024]{1,0:T(8,128)(2,1)S(1)}, bf16[128,1024]{1,0:T(8,128)(2,1)S(1)}, u32[]{:S(2)}, u32[]{:S(2)}) collective-permute-start(bf16[128,1024]{1,0:T(8,128)(2,1)S(1)} %shard_map.46.own), channel_id=1, source_target_pairs={{0,1},{1,0},{2,3},{3,2},{4,5},{5,4},{6,7},{7,6},{8,9},{9,8},{10,11... | collective-permute-start | bytes 786440 | tf_op jit(solution)/shard_map/ppermute | solution.py:238
  11.2 3.2 %collective-permute-start.2 = (bf16[128,1024]{1,0:T(8,128)(2,1)S(1)}, bf16[128,1024]{1,0:T(8,128)(2,1)S(1)}, u32[]{:S(2)}, u32[]{:S(2)}) collective-permute-start(bf16[128,1024]{1,0:T(8,128)(2,1)S(1)} %collective-permute-done.1.back), channel_id=1, source_target_pairs={{0,1},{1,0},{2,3},{3,2},{4,5},{5,4},{6,7},{7,6},{8,9},{9,8},{10,11... | collective-permute-start | bytes 786440 | tf_op jit(solution)/shard_map/ppermute | solution.py:238
  12.5 13.6 %collective-permute-start.5 = (bf16[128,1024]{1,0:T(8,128)(2,1)S(1)}, bf16[128,1024]{1,0:T(8,128)(2,1)S(1)}, u32[]{:S(2)}, u32[]{:S(2)}) collective-permute-start(bf16[128,1024]{1,0:T(8,128)(2,1)S(1)} %collective-permute-done.1.back), channel_id=1, source_target_pairs={{0,1},{1,0},{2,3},{3,2},{4,8},{5,9},{6,10},{7,11},{8,12},{9,13},{1... | collective-permute-start | bytes 786440 | tf_op jit(solution)/shard_map/ppermute | solution.py:238
  12.5 14.6 %collective-permute-start.6 = (bf16[128,1024]{1,0:T(8,128)(2,1)S(1)}, bf16[128,1024]{1,0:T(8,128)(2,1)S(1)}, u32[]{:S(2)}, u32[]{:S(2)}) collective-permute-start(bf16[128,1024]{1,0:T(8,128)(2,1)S(1)} %collective-permute-done.1.back), channel_id=1, source_target_pairs={{0,2},{1,3},{2,4},{3,5},{4,6},{5,7},{6,8},{7,9},{8,10},{9,11},{10,... | collective-permute-start | bytes 786440 | tf_op jit(solution)/shard_map/ppermute | solution.py:238
  13.7 12.4 %collective-permute-start.4 = (bf16[128,1024]{1,0:T(8,128)(2,1)S(1)}, bf16[128,1024]{1,0:T(8,128)(2,1)S(1)}, u32[]{:S(2)}, u32[]{:S(2)}) collective-permute-start(bf16[128,1024]{1,0:T(8,128)(2,1)S(1)} %collective-permute-done.3), channel_id=1, source_target_pairs={{0,4},{1,5},{2,3},{3,2},{4,8},{5,9},{6,7},{7,6},{8,12},{9,13},{10,... | collective-permute-start | bytes 786440 | tf_op jit(solution)/shard_map/ppermute | solution.py:238
  27.1 2.3 %collective-permute-start.8 = (bf16[128,1024]{1,0:T(8,128)(2,1)S(1)}, bf16[128,1024]{1,0:T(8,128)(2,1)S(1)}, u32[]{:S(2)}, u32[]{:S(2)}) collective-permute-start(bf16[128,1024]{1,0:T(8,128)(2,1)S(1)} %broadcast_select_fusion.refs_1_), channel_id=1, source_target_pairs={{0,1},{1,0},{2,3},{3,2},{4,5},{5,4},{6,7},{7,6},{8,9},{9,8},{10,11... | collective-permute-start | bytes 786440 | tf_op jit(solution)/shard_map/ppermute | solution.py:238
  27.9 1.5 %collective-permute-start.7 = (bf16[128,1024]{1,0:T(8,128)(2,1)S(1)}, bf16[128,1024]{1,0:T(8,128)(2,1)S(1)}, u32[]{:S(2)}, u32[]{:S(2)}) collective-permute-start(bf16[128,1024]{1,0:T(8,128)(2,1)S(1)} %collective-permute-done.6.refs_0_), channel_id=1, source_target_pairs={{0,1},{1,0},{2,3},{3,2},{4,5},{5,4},{6,7},{7,6},{8,9},{9,8},{10,11... | collective-permute-start | bytes 786440 | tf_op jit(solution)/shard_map/ppermute | solution.py:238
  28.0 1.8 %collective-permute-start.9 = (bf16[128,1024]{1,0:T(8,128)(2,1)S(1)}, bf16[128,1024]{1,0:T(8,128)(2,1)S(1)}, u32[]{:S(2)}, u32[]{:S(2)}) collective-permute-start(bf16[128,1024]{1,0:T(8,128)(2,1)S(1)} %collective-permute-done.5.refs_2_), channel_id=1, source_target_pairs={{0,1},{1,0},{2,3},{3,2},{4,5},{5,4},{6,7},{7,6},{8,9},{9,8},{10,11... | collective-permute-start | bytes 786440 | tf_op jit(solution)/shard_map/ppermute | solution.py:238
